TPU v7x, 128 devices: a whole 4x4x4 slice. The times are simulated.
128 devices in a mesh: group: 16 (over z, y_hi, core), tp: 8 (over y_lo, x).
Axes of the slice: x: 4, y: 4 (y_hi: 2, y_lo: 2; y = y_hi * 2 + y_lo), z: 4, core: 2. Of those that a mesh axis runs over, the one named last changes fastest.
Arguments:
- q_prefill: bfloat16 [16384, 8192], P('group', 'tp'), may hold values from -6 to 62
- kv_fresh: bfloat16 [2, 16384, 1024], P(None, 'group', 'tp'), may hold values from -6 to 42
- kv_pool: bfloat16 [2, 3328, 64, 1024], P(None, 'group', None, 'tp'), may hold values from -6 to 42
- block_table: int32 [208, 16], P('group'), may hold values from 0 to 207, as said below
- lengths: int32 [208], replicated, may hold values from 1 to 1024, as said below
- owners: int32 [192], replicated, may hold values from 0 to 15, as said below
- q_decode: bfloat16 [1024, 4, 8192], P('group', None, 'tp'), may hold values from -6 to 62
- kv_steps: bfloat16 [2, 1024, 4, 1024], P(None, 'group', None, 'tp'), may hold values from -6 to 42
- kv_resident: bfloat16 [2, 512, 2048, 256], P(None, 'group', 'tp'), may hold values from -6 to 42
- resident_len: int32 [512], P('group'), may hold values from 1 to 512, as said below
Outputs:
- prefill_out: bfloat16 [16384, 8192], P('group', 'tp')
- decode_out: bfloat16 [1024, 4, 8192], P('group', None, 'tp')
Inputs may be any that keep to these rules, and one draw needn't show every extreme that they name: `block_table`: each group's 12 + 1 rows (the last one for the prompt being prefilled) use each of that group's 208 blocks, numbered within the group, exactly once. In every group one of its 13 lengths is exactly 1024. `owners`: at most 2 of one group's finished requests go to one decode group; one decode group receives exactly 2 from every group. `resident_len`: in every group one request has exactly 512.
All inputs are finite; a program needn't handle non-finite values.
Results may differ from a plain program's by a relative error of at most 0.006.
Values may be sent and summed in bfloat16 or wider, within the bound.
A program may use at most 192 MiB of HBM per device.

v0:
```python
import jax
import jax.numpy as jnp
from jax import lax
from jax.sharding import PartitionSpec as P

Q_PER_KV = 8
HEAD_DIM = 128
MAXLEN = 1024
CAPACITY = 2


NEG_FILL = -1e30


def swapped(x, axis, stride):
    return lax.ppermute(x, axis, [(i, i ^ 1 << stride) for i in range(lax.axis_size(axis))])


def prefill_attention(queries, fresh_kv, ctx_kv, ctx_length, score_scale):
    row_count = queries.shape[0]
    head_count = queries.shape[1] // HEAD_DIM
    kv_count = fresh_kv.shape[2] // HEAD_DIM
    ctx_span = ctx_kv.shape[1]
    joined = jnp.concatenate([ctx_kv, fresh_kv], axis=1)
    key_span = joined.shape[1]
    joined = joined.reshape(2, key_span, kv_count, HEAD_DIM).transpose(2, 0, 1, 3)
    per_head = queries.reshape(row_count, head_count, HEAD_DIM).transpose(1, 0, 2)
    position = lax.broadcasted_iota(jnp.int32, (row_count, key_span), 1)
    token_idx = lax.broadcasted_iota(jnp.int32, (row_count, key_span), 0)
    usable = jnp.where(position < ctx_span, position < ctx_length, position - ctx_span <= token_idx)

    def one_head(head_item):
        query_rows, head_index = head_item
        kv_pair = joined[head_index // Q_PER_KV]
        scores = (
            jnp.einsum("id,ld->il", query_rows, kv_pair[0], preferred_element_type=jnp.float32)
            * score_scale
        )
        scores = jnp.where(usable, scores, NEG_FILL)
        row_max = jnp.max(scores, axis=-1, keepdims=True)
        expo_vals = jnp.exp(scores - row_max)
        normalizer = jnp.sum(expo_vals, axis=-1)
        weighted = jnp.dot(
            expo_vals.astype(jnp.bfloat16), kv_pair[1], preferred_element_type=jnp.float32
        )
        return (weighted / normalizer[:, None]).astype(jnp.bfloat16)

    head_outs = lax.map(one_head, (per_head, jnp.arange(head_count, dtype=jnp.int32)))
    return head_outs.transpose(1, 0, 2).reshape(row_count, head_count * HEAD_DIM)


def cache_scores(queries5, kv_cache, length_vec, offset, score_scale):
    row_count, key_span = (kv_cache.shape[1], kv_cache.shape[2])
    pair_heads = queries5.shape[2]
    key_rows = kv_cache[0].reshape(row_count, key_span, pair_heads, HEAD_DIM)
    scores = (
        jnp.einsum("rshqd,rlhd->rshql", queries5, key_rows, preferred_element_type=jnp.float32)
        * score_scale
    )
    position = offset + lax.broadcasted_iota(jnp.int32, (row_count, key_span), 1)
    usable = position < length_vec[:, None]
    return jnp.where(usable[:, None, None, None, :], scores, NEG_FILL)


def cache_terms(scores, kv_cache, row_max):
    row_count, key_span = (kv_cache.shape[1], kv_cache.shape[2])
    pair_heads = scores.shape[2]
    values = kv_cache[1].reshape(row_count, key_span, pair_heads, HEAD_DIM)
    expo_vals = jnp.exp(scores - row_max[..., None])
    normalizer = jnp.sum(expo_vals, axis=-1)
    weighted = jnp.einsum(
        "rshql,rlhd->rshqd",
        expo_vals.astype(jnp.bfloat16),
        values,
        preferred_element_type=jnp.float32,
    )
    return (weighted, normalizer)


def pair_join(pair_side, own_part, other_part):
    return jnp.where(
        pair_side == 0,
        jnp.concatenate([own_part, other_part], axis=-1),
        jnp.concatenate([other_part, own_part], axis=-1),
    )


def per_device(
    q_prefill,
    kv_fresh,
    kv_pool,
    block_table,
    lengths,
    owners,
    q_decode,
    kv_steps,
    kv_resident,
    resident_len,
):
    groups = lax.axis_size("group")
    own_group = lax.axis_index("group")
    pair_side = lax.axis_index("tp") % 2
    finished = owners.shape[0] // groups
    score_scale = HEAD_DIM ** (-0.5)
    own_heads = kv_fresh.shape[2] // HEAD_DIM
    width_own = own_heads * HEAD_DIM
    half_len = MAXLEN // 2
    new_rows = groups * CAPACITY
    ctx_blocks = block_table[finished]
    ctx_kv = kv_pool[:, ctx_blocks].reshape(2, MAXLEN, width_own)
    ctx_length = lengths[own_group * (finished + 1) + finished]
    prefill_out = prefill_attention(q_prefill, kv_fresh, ctx_kv, ctx_length, score_scale)
    owner_table = owners.reshape(groups, finished)
    same_owner = owner_table[:, :, None] == owner_table[:, None, :]
    earlier = lax.broadcasted_iota(jnp.int32, (finished, finished), 1) < lax.broadcasted_iota(
        jnp.int32, (finished, finished), 0
    )
    arrival_rank = jnp.sum((same_owner & earlier[None]).astype(jnp.int32), axis=2)
    dest_slot = owner_table[own_group] * CAPACITY + arrival_rank[own_group]
    slot_ids = jnp.arange(new_rows, dtype=jnp.int32)
    sender_match = slot_ids[:, None] == dest_slot[None, :]
    present = jnp.any(sender_match, axis=1)
    source = jnp.sum(
        jnp.where(sender_match, jnp.arange(finished, dtype=jnp.int32)[None, :], 0), axis=1
    )
    slot_table = jnp.arange(groups, dtype=jnp.int32)[:, None] * CAPACITY + arrival_rank
    arriving = (owner_table == own_group)[None] & (slot_table[None] == slot_ids[:, None, None])
    fin_lengths = lengths.reshape(groups, finished + 1)[:, :finished]
    new_length = jnp.sum(jnp.where(arriving, fin_lengths[None], 0), axis=(1, 2))
    fin_data = kv_pool[:, block_table[:finished]].reshape(2, finished, MAXLEN, width_own)
    q_partner = swapped(q_decode, "tp", 0)
    picked = jnp.take(fin_data, source, axis=1)
    picked = jnp.where(present[None, :, None, None], picked, jnp.zeros_like(picked))
    arrived = lax.all_to_all(
        picked.reshape(2, groups, CAPACITY, fin_data.shape[2], fin_data.shape[3]),
        "group",
        split_axis=1,
        concat_axis=1,
        tiled=True,
    )
    arrived = arrived.reshape(2, new_rows, MAXLEN, width_own)
    handed = jnp.where(pair_side == 0, arrived[:, :, half_len:], arrived[:, :, :half_len])
    retained = jnp.where(pair_side == 0, arrived[:, :, :half_len], arrived[:, :, half_len:])
    received = swapped(handed, "tp", 0)
    new_cache = pair_join(pair_side, retained, received)
    row_count = q_decode.shape[0]
    steps = q_decode.shape[1]
    resident_rows = kv_resident.shape[1]
    q_pair = pair_join(pair_side, q_decode, q_partner).reshape(
        row_count, steps, 2 * own_heads, Q_PER_KV, HEAD_DIM
    )
    res_scores = cache_scores(
        q_pair[:resident_rows],
        kv_resident,
        resident_len,
        pair_side * kv_resident.shape[2],
        score_scale,
    )
    new_scores = cache_scores(
        q_pair[resident_rows:], new_cache, new_length, pair_side * half_len, score_scale
    )
    own_query = q_decode.reshape(row_count, steps, own_heads, Q_PER_KV, HEAD_DIM)
    step_keys = kv_steps[0].reshape(row_count, steps, own_heads, HEAD_DIM)
    step_values = kv_steps[1].reshape(row_count, steps, own_heads, HEAD_DIM)
    step_scores = (
        jnp.einsum("rshqd,rthd->rshqt", own_query, step_keys, preferred_element_type=jnp.float32)
        * score_scale
    )
    causal = lax.broadcasted_iota(jnp.int32, (steps, steps), 1) <= lax.broadcasted_iota(
        jnp.int32, (steps, steps), 0
    )
    step_scores = jnp.where(causal[None, :, None, None, :], step_scores, NEG_FILL)
    cache_max = jnp.concatenate(
        [jnp.max(res_scores, axis=-1), jnp.max(new_scores, axis=-1)], axis=0
    )
    step_max = jnp.max(step_scores, axis=-1)
    filler = jnp.full_like(step_max, NEG_FILL)
    step_full = jnp.where(
        pair_side == 0,
        jnp.concatenate([step_max, filler], axis=2),
        jnp.concatenate([filler, step_max], axis=2),
    )
    local_max = jnp.maximum(cache_max, step_full)
    other_max = swapped(local_max, "tp", 0)
    row_max = jnp.maximum(local_max, other_max)
    res_weighted, res_norm = cache_terms(res_scores, kv_resident, row_max[:resident_rows])
    new_weighted, new_norm = cache_terms(new_scores, new_cache, row_max[resident_rows:])
    weighted = jnp.concatenate([res_weighted, new_weighted], axis=0)
    normalizer = jnp.concatenate([res_norm, new_norm], axis=0)
    own_max = jnp.where(pair_side == 0, row_max[:, :, :own_heads], row_max[:, :, own_heads:])
    step_exp = jnp.exp(step_scores - own_max[..., None])
    step_norm = jnp.sum(step_exp, axis=-1)
    step_weighted = jnp.einsum(
        "rshqt,rthd->rshqd",
        step_exp.astype(jnp.bfloat16),
        step_values,
        preferred_element_type=jnp.float32,
    )
    kept_weighted = (
        jnp.where(pair_side == 0, weighted[:, :, :own_heads], weighted[:, :, own_heads:])
        + step_weighted
    )
    kept_norm = (
        jnp.where(pair_side == 0, normalizer[:, :, :own_heads], normalizer[:, :, own_heads:])
        + step_norm
    )
    given_weighted = jnp.where(
        pair_side == 0, weighted[:, :, own_heads:], weighted[:, :, :own_heads]
    )
    given_norm = jnp.where(
        pair_side == 0, normalizer[:, :, own_heads:], normalizer[:, :, :own_heads]
    )
    got_weighted, got_norm = (
        swapped(given_weighted.astype(jnp.bfloat16), "tp", 0).astype(given_weighted.dtype),
        swapped(given_norm.astype(jnp.bfloat16), "tp", 0).astype(given_norm.dtype),
    )
    decode_out = ((kept_weighted + got_weighted) / (kept_norm + got_norm)[..., None]).astype(
        jnp.bfloat16
    )
    decode_out = decode_out.reshape(row_count, steps, own_heads * Q_PER_KV * HEAD_DIM)
    return (prefill_out, decode_out)


def solution(mesh):
    in_specs = (
        P("group", "tp"),
        P(None, "group", "tp"),
        P(None, "group", None, "tp"),
        P("group", None),
        P(),
        P(),
        P("group", None, "tp"),
        P(None, "group", None, "tp"),
        P(None, "group", "tp", None),
        P("group"),
    )
    out_specs = (P("group", "tp"), P("group", None, "tp"))
    return jax.shard_map(
        per_device, mesh=mesh, in_specs=in_specs, out_specs=out_specs, check_vma=False
    )
```

profile of v0, /device:TPU:1, one launch (start us, length us, event | category | flops | bytes accessed | tf_op | source)
XLA Modules:
  0.0 519.4 jit_solution(3204647909462794731)
XLA Ops:
  3.1 11.0 %gather_fusion.1 = bf16[192,2,64,128]{3,2,1,0:T(8,128)(2,1)} fusion(bf16[2,208,64,128]{3,2,1,0:T(8,128)(2,1)} %param.14, s32[1024]{0:T(1024)S(1)} %pad_clamp_fusion.1), kind=kCustom, calls=%fused_computation.1 | custom fusion | bytes 12583680 | tf_op jit(solution)/shard_map/gather | solution.py:130
  14.1 7.3 %copy.112 = bf16[192,2,64,128]{3,2,0,1:T(8,128)(2,1)} copy(bf16[192,2,64,128]{3,2,1,0:T(8,128)(2,1)} %gather_fusion.1) | data formatting | bytes 12582912 | tf_op jit(solution)/shard_map/gather | solution.py:130
  21.5 9.9 %gather_fusion.2 = bf16[32,2,1024,128]{3,2,1,0:T(8,128)(2,1)} fusion(bf16[2,12,1024,128]{3,2,1,0:T(8,128)(2,1)} %bitcast.157, s32[1024]{0:T(1024)S(1)} %pad_clamp_fusion), kind=kCustom, calls=%fused_computation.2 | custom fusion | bytes 33554560 | tf_op jit(solution)/shard_map/jit(_take)/gather | solution.py:132
  31.5 14.3 %select_select_fusion = bf16[2,16,2,1024,128]{4,3,0,2,1:T(8,128)(2,1)} fusion(bf16[2,16,2,1024,128]{4,3,0,2,1:T(8,128)(2,1)} %bitcast.158, pred[16,2]{1,0:T(8,128)(4,1)S(1)} %compare_and_fusion, pred[16,2]{1,0:T(8,128)(4,1)S(1)} %broadcast_in_dim.128), kind=kLoop, calls=%fused_computation.27 | loop fusion | flops 16777216 | bytes 33554496 | tf_op jit(solution)/shard_map/jit(_where)/select_n | solution.py:133
  45.8 9.7 %all-to-all-start = ((bf16[2,16,2,1024,128]{4,3,0,2,1:T(8,128)(2,1)}), bf16[2,16,2,1024,128]{4,3,0,2,1:T(8,128)(2,1)}, u32[]{:S(2)}, u32[]{:S(2)}) async-start(bf16[2,16,2,1024,128]{4,3,0,2,1:T(8,128)(2,1)} %select_select_fusion), calls=%async_computation | async-start | bytes 33554432 | tf_op jit(solution)/shard_map/all_to_all | solution.py:134
  57.5 3.6 gather_fusion
  67.8 173.6 %all-to-all-done = bf16[2,16,2,1024,128]{4,3,0,2,1:T(8,128)(2,1)} async-done(((bf16[2,16,2,1024,128]{4,3,0,2,1:T(8,128)(2,1)}), bf16[2,16,2,1024,128]{4,3,0,2,1:T(8,128)(2,1)}, u32[]{:S(2)}, u32[]{:S(2)}) %all-to-all-start) | async-done | bytes 16777248 | tf_op jit(solution)/shard_map/all_to_all | solution.py:134
  241.4 22.4 %copy.113 = bf16[2,16,2,1024,128]{3,4,2,1,0:T(8,128)(2,1)} copy(bf16[2,16,2,1024,128]{4,3,0,2,1:T(8,128)(2,1)} %all-to-all-done) | data formatting | bytes 33554432 | tf_op jit(solution)/shard_map/all_to_all | solution.py:134
  263.8 11.5 %broadcast_select_fusion.1 = (bf16[2,32,512,128]{2,3,1,0:T(8,128)(2,1)}, bf16[2,32,512,128]{2,3,1,0:T(8,128)(2,1)}) fusion(pred[]{:T(512)S(6)} %eq.32, bf16[2,32,1024,128]{2,3,1,0:T(8,128)(2,1)} %bitcast.159), kind=kLoop, calls=%fused_computation.29 | loop fusion | flops 8388608 | bytes 33554432 | tf_op jit(solution)/shard_map/jit(_where)/select_n | solution.py:143
  276.5 83.4 %while.12 = (s32[]{:T(128)}, bf16[8,1024,128]{2,1,0:T(8,128)(2,1)S(1)}, bf16[8,1024,128]{1,2,0:T(8,128)(2,1)}, bf16[1,2,2048,128]{3,2,1,0:T(8,128)(2,1)}, s32[20...) while((s32[]{:T(128)}, ...), condition=%wide.region_3.4_spmd.clone, body=%wide.region_0.3_spmd.clone.sunk | while | flops 1109653504 | bytes 30990964 | solution.py:48
  276.5 3.7 fusion.97
  280.2 3.5 fusion.98
  286.9 3.7 fusion.97
  297.3 3.7 fusion.97
  301.1 3.5 fusion.98
  307.8 3.7 fusion.97
  318.2 3.7 fusion.97
  321.9 3.5 fusion.98
  328.6 3.7 fusion.97
  332.4 3.5 fusion.98
  339.0 3.7 fusion.97
  342.8 3.5 fusion.98
  349.5 3.7 fusion.97
  360.4 6.1 %fusion.80 = (bf16[1,32,256,256]{3,2,1,0:T(8,128)(2,1)}, bf16[1,32,256,256]{3,2,1,0:T(8,128)(2,1)}) fusion(bf16[2,32,256,256]{3,2,1,0:T(8,128)(2,1)} %param.20), kind=kLoop, calls=%fused_computation.126 | loop fusion | bytes 16777216 | tf_op jit(solution)/shard_map/slice | solution.py:68
  366.8 6.4 %copy.145 = bf16[1,32,256,256]{2,3,1,0:T(8,128)(2,1)} copy(bf16[1,32,256,256]{3,2,1,0:T(8,128)(2,1)} %get-tuple-element.119) | data formatting | bytes 8388608
  382.9 73.7 %collective-permute-done.1 = bf16[2,32,512,128]{2,3,1,0:T(8,128)(2,1)} collective-permute-done((bf16[2,32,512,128]{2,3,1,0:T(8,128)(2,1)}, bf16[2,32,512,128]{2,3,1,0:T(8,128)(2,1)}, u32[]{:S(2)}, u32[]{:S(2)}) %collective-permute-start.1) | collective-permute-done | bytes 8388640 | tf_op jit(solution)/shard_map/ppermute | solution.py:16
  456.6 17.8 %maximum_select_fusion = bf16[2,32,512,256]{2,3,1,0:T(8,128)(2,1)S(1)} fusion(bf16[2,32,512,128]{2,3,1,0:T(8,128)(2,1)} %collective-permute-done.1, bf16[2,32,512,128]{2,3,1,0:T(8,128)(2,1)} %get-tuple-element.116, pred[]{:T(512)S(6)} %eq.32), kind=kLoop, calls=%fused_computation.26 | loop fusion | flops 75497472 | bytes 33554432 | tf_op jit(solution)/shard_map/jit(_where)/select_n | solution.py:81
  474.4 4.4 fusion.79
  485.4 6.4 %copy.146 = bf16[1,32,256,256]{2,3,1,0:T(8,128)(2,1)} copy(bf16[1,32,256,256]{3,2,1,0:T(8,128)(2,1)} %get-tuple-element.118) | data formatting | bytes 8388608
  497.3 3.8 convolution_bitcast_fusion.1
  501.2 5.6 %fusion.42 = f32[32,4,2,8,128]{4,3,1,2,0:T(8,128)S(1)} fusion(bf16[32,512,2,128,1]{1,3,4,2,0:T(8,128)(2,1)} %bitcast.162, f32[32,2,512,4,8]{2,4,3,1,0:T(8,128)S(1)} %copy-done, f32[32,4,2,8]{3,1,2,0:T(4,128)S(1)} %get-tuple-element.123, pred[32,512]{1,0:T(8,128)(4,1)S(1)} %copy-done.11), kind=kOutput, calls=%fused_computation.50 | convolution fusion | flops 272629760 | bytes 13656064 | tf_op jit(solution)/shard_map/rshql,rlhd->rshqd/dot_general | solution.py:71
  508.6 9.3 %collective-permute-done.3 = bf16[64,4,1,8,128]{4,3,1,2,0:T(8,128)(2,1)S(1)} collective-permute-done((bf16[64,4,1,8,128]{4,3,1,2,0:T(8,128)(2,1)S(1)}, bf16[64,4,1,8,128]{4,3,1,2,0:T(8,128)(2,1)S(1)}, u32[]{:S(2)}, u32[]{:S(2)}) %collective-permute-start.3) | collective-permute-done | bytes 524320 | tf_op jit(solution)/shard_map/ppermute | solution.py:16
  (127 shorter events, 73.9 us)
Async XLA Ops:
  45.7 9.7 %copy-start.1 = (bf16[64,4,1024]{2,1,0:T(4,128)(2,1)S(1)}, bf16[64,4,1024]{2,1,0:T(4,128)(2,1)}, u32[]{:S(2)}) copy-start(bf16[64,4,1024]{2,1,0:T(4,128)(2,1)} %param.18) | copy-start | bytes 1572868
  45.7 16.2 %copy-start.2 = (bf16[1024,1024]{1,0:T(8,128)(2,1)S(1)}, bf16[1024,1024]{1,0:T(8,128)(2,1)}, u32[]{:S(2)}) copy-start(bf16[1024,1024]{1,0:T(8,128)(2,1)} %param.12) | copy-start | bytes 6291460
  45.8 195.6 %all-to-all-start = ((bf16[2,16,2,1024,128]{4,3,0,2,1:T(8,128)(2,1)}), bf16[2,16,2,1024,128]{4,3,0,2,1:T(8,128)(2,1)}, u32[]{:S(2)}, u32[]{:S(2)}) async-start(bf16[2,16,2,1024,128]{4,3,0,2,1:T(8,128)(2,1)} %select_select_fusion), calls=%async_computation | async-start | bytes 33554432 | tf_op jit(solution)/shard_map/all_to_all | solution.py:134
  55.5 9.0 %copy-start.12 = (s32[208]{0:T(256)S(1)}, s32[208]{0:T(256)}, u32[]{:S(2)}) copy-start(s32[208]{0:T(256)} %param.16) | copy-start | bytes 2500
  55.5 320.2 %collective-permute-start = (bf16[64,4,1024]{2,1,0:T(4,128)(2,1)S(1)}, bf16[64,4,1024]{2,1,0:T(4,128)(2,1)}, u32[]{:S(2)}, u32[]{:S(2)}) collective-permute-start(bf16[64,4,1024]{2,1,0:T(4,128)(2,1)S(1)} %copy-done.1), channel_id=1, source_target_pairs={{0,1},{1,0},{2,3},{3,2},{4,5},{5,4},{6,7},{7,6},{8,9},{9,8},{10,11... | collective-permute-start | bytes 1572872 | tf_op jit(solution)/shard_map/ppermute | solution.py:16
  61.9 3.7 copy-start.6
  263.8 12.7 %copy-start.3 = (bf16[8,1024,128]{2,1,0:T(8,128)(2,1)S(1)}, bf16[8,1024,128]{2,1,0:T(8,128)(2,1)}, u32[]{:S(2)}) copy-start(bf16[8,1024,128]{2,1,0:T(8,128)(2,1)} %custom-call.6) | copy-start | bytes 6291460
  275.3 181.4 %collective-permute-start.1 = (bf16[2,32,512,128]{2,3,1,0:T(8,128)(2,1)}, bf16[2,32,512,128]{2,3,1,0:T(8,128)(2,1)}, u32[]{:S(2)}, u32[]{:S(2)}) collective-permute-start(bf16[2,32,512,128]{2,3,1,0:T(8,128)(2,1)} %get-tuple-element.117), channel_id=1, source_target_pairs={{0,1},{1,0},{2,3},{3,2},{4,5},{5,4},{6,7},{7,6},{8,9},{9,8},{10,11... | collective-permute-start | bytes 25165832 | tf_op jit(solution)/shard_map/ppermute | solution.py:16
  276.5 83.9 %copy-start.13 = (s32[32]{0:T(128)S(1)}, s32[32]{0:T(128)}, u32[]{:S(2)}) copy-start(s32[32]{0:T(128)} %param.21) | copy-start | bytes 388
  280.2 3.5 copy-start.7
  290.6 3.5 copy-start.7
  301.1 3.5 copy-start.7
  311.5 3.5 copy-start.7
  321.9 3.5 copy-start.7
  332.4 3.5 copy-start.7
  342.8 3.5 copy-start.7
  353.2 3.5 copy-start.7
  359.9 6.7 %copy-start.4 = (bf16[8,1024,128]{2,1,0:T(8,128)(2,1)}, bf16[8,1024,128]{2,1,0:T(8,128)(2,1)S(1)}, u32[]{:S(2)}) copy-start(bf16[8,1024,128]{2,1,0:T(8,128)(2,1)S(1)} %get-tuple-element.43) | copy-start | bytes 6291460
  366.8 6.5 %copy-start.14 = (bf16[2,64,4,128]{3,2,1,0:T(4,128)(2,1)S(1)}, bf16[2,64,4,128]{3,2,1,0:T(4,128)(2,1)}, u32[]{:S(2)}) copy-start(bf16[2,64,4,128]{3,2,1,0:T(4,128)(2,1)} %param.19) | copy-start | bytes 393220
  373.3 105.5 %copy-start.9 = (pred[32,512]{1,0:T(8,128)(4,1)}, pred[32,512]{1,0:T(8,128)(4,1)S(1)}, u32[]{:S(2)}) copy-start(pred[32,512]{1,0:T(8,128)(4,1)S(1)} %broadcast_compare_fusion) | copy-start | bytes 49156
  474.4 4.4 copy-start.8
  478.8 4.9 copy-start.5
  482.5 9.3 %collective-permute-start.2 = (f32[64,4,2,8]{3,1,2,0:T(4,128)S(1)}, f32[64,4,2,8]{3,1,2,0:T(4,128)S(1)}, u32[]{:S(2)}, u32[]{:S(2)}) collective-permute-start(f32[64,4,2,8]{3,1,2,0:T(4,128)S(1)} %maximum_maximum_fusion), channel_id=1, source_target_pairs={{0,1},{1,0},{2,3},{3,2},{4,5},{5,4},{6,7},{7,6},{8,9},{9,8},{10,11... | collective-permute-start | bytes 49160 | tf_op jit(solution)/shard_map/ppermute | solution.py:16
  485.4 6.5 %copy-start.10 = (pred[32,512]{1,0:T(8,128)(4,1)S(1)}, pred[32,512]{1,0:T(8,128)(4,1)}, u32[]{:S(2)}) copy-start(pred[32,512]{1,0:T(8,128)(4,1)} %copy-done.9) | copy-start | bytes 49156
  496.5 4.7 copy-start.11
  496.9 4.3 copy-start
  497.0 11.5 %collective-permute-start.4 = (bf16[64,4,1,8]{3,1,2,0:T(4,128)(2,1)S(1)}, bf16[64,4,1,8]{3,1,2,0:T(4,128)(2,1)S(1)}, u32[]{:S(2)}, u32[]{:S(2)}) collective-permute-start(bf16[64,4,1,8]{3,1,2,0:T(4,128)(2,1)S(1)} %select_convert_fusion.1), channel_id=1, source_target_pairs={{0,1},{1,0},{2,3},{3,2},{4,5},{5,4},{6,7},{7,6},{8,9},{9,8},{10,11... | collective-permute-start | bytes 12296 | tf_op jit(solution)/shard_map/ppermute | solution.py:16
  506.8 11.1 %copy-start.15 = (bf16[2,64,4,128]{3,2,1,0:T(4,128)(2,1)S(1)}, bf16[2,64,4,128]{3,2,1,0:T(4,128)(2,1)}, u32[]{:S(2)}) copy-start(bf16[2,64,4,128]{3,2,1,0:T(4,128)(2,1)} %param.19) | copy-start | bytes 393220
  506.9 11.0 %collective-permute-start.3 = (bf16[64,4,1,8,128]{4,3,1,2,0:T(8,128)(2,1)S(1)}, bf16[64,4,1,8,128]{4,3,1,2,0:T(8,128)(2,1)S(1)}, u32[]{:S(2)}, u32[]{:S(2)}) collective-permute-start(bf16[64,4,1,8,128]{4,3,1,2,0:T(8,128)(2,1)S(1)} %select_convert_fusion), channel_id=1, source_target_pairs={{0,1},{1,0},{2,3},{3,2},{4,5},{5,4},{6,7},{7,6},{8,9},{9,8},{10,11... | collective-permute-start | bytes 1572872 | tf_op jit(solution)/shard_map/ppermute | solution.py:16
where the time goes:
time: 523 us; the launch traced here: 519 us
  waiting for transfers between devices  257 us (49%)
  local copies, waits for them, and re-layouts  88.1 us (17%)
  other arithmetic  84.4 us (16%)
  matrix products  74.1 us (14%)
  starting transfers between devices  15 us (3%)
    all_to_all x1, waiting for transfers between devices, per_device(): lax.all_to_all(picked.reshape(2, groups, CAPACITY, fin_data.shape[2], fin...  174 us
    ppermute x5, waiting for transfers between devices, swapped(): lax.ppermute(x, axis, [(i, i ^ 1 << stride) for i in range(lax.axis_size(...  83 us
    dot_general x8, matrix products, one_head(): jnp.einsum('id,ld->il', query_rows, kv_pair[0], preferred_element_type=jn...  29.9 us
    reduce_sum x8, other arithmetic, one_head(): normalizer = jnp.sum(expo_vals, axis=-1)  28 us
    dot_general x8, matrix products, one_head(): jnp.dot(expo_vals.astype(jnp.bfloat16), kv_pair[1], preferred_element_typ...  25.1 us
    all_to_all x1, local copies, waits for them, and re-layouts, per_device(): lax.all_to_all(picked.reshape(2, groups, CAPACITY, fin_data.shape[2], fin...  22.4 us
    select_n x2, other arithmetic, pair_join(): jnp.where(pair_side == 0, jnp.concatenate([own_part, other_part], axis=-1...  19.9 us
    gather x2, local copies, waits for them, and re-layouts, per_device(): kv_pool[:, block_table[:finished]].reshape(2, finished, MAXLEN, width_own)  18.3 us
  transfers between devices with their start and end apart: 6, of which 3 were waited for; matrix products, arithmetic and copies ran while one was open for 33% of the time, Pallas kernels for 0%

commit v1 on v0

v1 whole, which is shorter than its diff:
```python
import functools

import jax
import jax.numpy as jnp
from jax import lax
from jax.experimental import pallas as pl
from jax.experimental.pallas import tpu as pltpu
from jax.sharding import PartitionSpec as P

HEAD_DIM = 128
Q_PER_KV = 8
MAXLEN = 1024
CAPACITY = 2
NEG_FILL = -1e30
SCALE = HEAD_DIM ** -0.5 * 1.4426950408889634
PACK = 96
TILE = 128
STACK = 4
MESH = pl.DeviceIdType.MESH
BF16 = jnp.bfloat16
F32 = jnp.float32


def dot_nt(a, b):
    return lax.dot_general(a, b, (((1,), (1,)), ((), ())), preferred_element_type=F32)


def dot_nn(a, b):
    return jnp.dot(a, b, preferred_element_type=F32)


def heads_to_rows(x):
    wide = x.astype(F32)
    parts = [wide[:, a * HEAD_DIM:(a + 1) * HEAD_DIM] for a in range(Q_PER_KV)]
    return jnp.concatenate(parts, axis=0).astype(BF16)


def kernel(
    groups,
    qp_hbm,
    fresh_hbm,
    pool_hbm,
    table,
    lengths,
    owners,
    qd_hbm,
    steps_hbm,
    res_hbm,
    res_len,
    pout_hbm,
    dout_hbm,
    qp,
    fresh,
    pool,
    qd,
    steps,
    res,
    pout,
    dout,
    kbuf,
    vbuf,
    diag,
    q_own,
    q_partner,
    pack_send,
    pack_recv,
    ks_res,
    ks_arr,
    step_only,
    ans,
    ans_send,
    ans_recv,
    part_send,
    part_recv,
    stat_send,
    stat_recv,
    own_part,
    own_stat,
    load_sem,
    out_sem,
    pack_send_sem,
    pack_recv_sem,
    ans_send_sem,
    ans_recv_sem,
    pair_send_sem,
    pair_recv_sem,
):
    me = lax.axis_index("group")
    tp = lax.axis_index("tp")
    side = tp % 2
    partner = tp + 1 - 2 * side
    finished = owners.shape[0] // groups
    res_rows = res.shape[1]
    span_res = res.shape[2]
    n_step = qd.shape[1]
    q_rows = Q_PER_KV * n_step
    seg = qp.shape[0]

    barrier = pltpu.get_barrier_semaphore()

    def greet(d, carry):
        pl.semaphore_signal(
            barrier, inc=1, device_id={"group": (me + d) % groups}, device_id_type=MESH
        )
        return carry

    lax.fori_loop(1, groups, greet, 0)
    pl.semaphore_signal(barrier, inc=1, device_id={"tp": partner}, device_id_type=MESH)

    loads = [
        pltpu.make_async_copy(qd_hbm, qd, load_sem.at[0]),
        pltpu.make_async_copy(steps_hbm, steps, load_sem.at[1]),
        pltpu.make_async_copy(fresh_hbm, fresh, load_sem.at[2]),
        pltpu.make_async_copy(pool_hbm, pool, load_sem.at[3]),
        pltpu.make_async_copy(qp_hbm, qp, load_sem.at[4]),
        pltpu.make_async_copy(res_hbm, res, load_sem.at[5]),
    ]
    for one in loads:
        one.start()

    loads[0].wait()
    loads[1].wait()

    def relay_res(r, carry):
        q_own[r] = heads_to_rows(qd[r])
        return carry

    lax.fori_loop(0, res_rows, relay_res, 0, unroll=4)

    def relay_arr(o, carry):
        first = res_rows + o * CAPACITY
        for c in range(CAPACITY):
            pack_send[o, c * q_rows:(c + 1) * q_rows] = heads_to_rows(qd[first + c])
        for k in range(2):
            rows = [steps[k, first + c].astype(F32) for c in range(CAPACITY)]
            rows.append(jnp.zeros((16 - CAPACITY * n_step, HEAD_DIM), F32))
            start = CAPACITY * q_rows + 16 * k
            pack_send[o, start:start + 16] = jnp.concatenate(rows, axis=0).astype(BF16)
        return carry

    lax.fori_loop(0, groups, relay_arr, 0, unroll=2)

    pl.semaphore_wait(barrier, groups)

    def pack_copy(peer):
        return pltpu.make_async_remote_copy(
            src_ref=pack_send.at[peer],
            dst_ref=pack_recv.at[me],
            send_sem=pack_send_sem.at[peer],
            recv_sem=pack_recv_sem.at[me],
            device_id={"group": peer},
            device_id_type=MESH,
        )

    def pair_copy(src, dst, i):
        return pltpu.make_async_remote_copy(
            src_ref=src,
            dst_ref=dst,
            send_sem=pair_send_sem.at[i],
            recv_sem=pair_recv_sem.at[i],
            device_id={"tp": partner},
            device_id_type=MESH,
        )

    q_pair = pair_copy(q_own, q_partner, 0)
    q_pair.start()

    def send_pack(d, carry):
        pack_copy((me + d) % groups).start()
        return carry

    lax.fori_loop(1, groups, send_pack, 0)
    pack_recv[me] = pack_send[me]

    per_tile = 16 // n_step

    def gather_steps(i, carry):
        for k in range(2):
            for base, dst in ((0, ks_res), (res_rows, ks_arr)):
                rows = [steps[k, base + i * per_tile + c].astype(F32) for c in range(per_tile)]
                dst[k, pl.ds(pl.multiple_of(i * 16, 16), 16)] = jnp.concatenate(
                    rows, axis=0
                ).astype(BF16)
        return carry

    lax.fori_loop(0, res_rows // per_tile, gather_steps, 0, unroll=2)

    loads[2].wait()
    loads[3].wait()
    ctx_len = lengths[me * (finished + 1) + finished]
    first_key = pool[0, table[finished, 0]][0:1]
    block = pool.shape[2]
    for b in range(MAXLEN // block):
        blk = table[finished, b]
        valid = lax.broadcasted_iota(jnp.int32, (block, HEAD_DIM), 0) + b * block < ctx_len
        kbuf[b * block:(b + 1) * block] = jnp.where(
            valid, pool[0, blk].astype(F32), first_key.astype(F32)
        ).astype(BF16)
        vbuf[b * block:(b + 1) * block, :HEAD_DIM] = jnp.where(
            valid, pool[1, blk].astype(F32), 0.0
        ).astype(BF16)
        vbuf[b * block:(b + 1) * block, HEAD_DIM:] = jnp.where(valid, 1.0, 0.0).astype(BF16)
    kbuf[MAXLEN:] = fresh[0]
    vbuf[MAXLEN:, :HEAD_DIM] = fresh[1]
    vbuf[MAXLEN:, HEAD_DIM:] = jnp.ones((seg, HEAD_DIM), BF16)
    row = lax.broadcasted_iota(jnp.int32, (STACK * TILE, TILE), 0) % TILE
    col = lax.broadcasted_iota(jnp.int32, (STACK * TILE, TILE), 1)
    diag[...] = jnp.where(col <= row, 0.0, NEG_FILL)
    loads[4].wait()

    def prefill(first_head):
        cols = [slice((first_head + h) * HEAD_DIM, (first_head + h + 1) * HEAD_DIM) for h in range(STACK)]
        for i in range(seg // TILE):
            rows = slice(i * TILE, (i + 1) * TILE)
            span = MAXLEN + (i + 1) * TILE
            q = jnp.concatenate([qp[rows, c] for c in cols], axis=0)
            s = dot_nt(q, kbuf[:span])
            s = jnp.concatenate([s[:, :span - TILE], s[:, span - TILE:] + diag[...]], axis=1)
            top = jnp.max(s, axis=1, keepdims=True)
            p = jnp.exp2(s * SCALE - top * SCALE).astype(BF16)
            o = dot_nn(p, vbuf[:span])
            o = (o[:, :HEAD_DIM] / o[:, HEAD_DIM:]).astype(BF16)
            for h in range(STACK):
                pout[rows, cols[h]] = o[h * TILE:(h + 1) * TILE]

    prefill(0)
    half = STACK * HEAD_DIM
    out_first = pltpu.make_async_copy(
        pout.at[:, pl.ds(0, half)], pout_hbm.at[:, pl.ds(0, half)], out_sem.at[0]
    )
    out_first.start()

    loads[5].wait()
    q_pair.wait()
    lane = lax.broadcasted_iota(jnp.int32, (q_rows, HEAD_DIM), 1)
    position = side * span_res + lax.broadcasted_iota(jnp.int32, (q_rows, span_res), 1)

    def partner_rows(r, carry):
        tops, norms = carry
        cols = pl.ds(pl.multiple_of((1 - side) * HEAD_DIM, HEAD_DIM), HEAD_DIM)
        s = dot_nt(q_partner[r], res[0, r, :, cols])
        s = jnp.where(position < res_len[r], s * SCALE, NEG_FILL)
        top = jnp.max(s, axis=1, keepdims=True)
        p = jnp.exp2(s - top)
        norm = jnp.sum(p, axis=1, keepdims=True)
        part_send[r] = dot_nn(p.astype(BF16), res[1, r, :, cols]).astype(BF16)
        return jnp.where(lane == r, top, tops), jnp.where(lane == r, norm, norms)

    zeros = jnp.zeros((q_rows, HEAD_DIM), F32)
    tops, norms = lax.fori_loop(0, res_rows, partner_rows, (zeros, zeros), unroll=4)
    stat_send[0] = tops
    stat_send[1] = norms
    part_pair = pair_copy(part_send, part_recv, 1)
    part_pair.start()
    stat_pair = pair_copy(stat_send, stat_recv, 2)
    stat_pair.start()

    def wait_pack(d, carry):
        peer = (me + d) % groups
        pltpu.make_async_remote_copy(
            src_ref=pack_send.at[peer],
            dst_ref=pack_recv.at[peer],
            send_sem=pack_send_sem.at[peer],
            recv_sem=pack_recv_sem.at[peer],
            device_id={"group": peer},
            device_id_type=MESH,
        ).wait()
        return carry

    lax.fori_loop(1, groups, wait_pack, 0)

    owner_of = [owners[me * finished + f] for f in range(finished)]
    slot_of = []
    for f in range(finished):
        rank = jnp.int32(0)
        for f2 in range(f):
            rank = rank + jnp.where(owner_of[f2] == owner_of[f], 1, 0)
        slot_of.append(owner_of[f] * CAPACITY + rank)

    cache_pos = lax.broadcasted_iota(jnp.int32, (q_rows, MAXLEN), 1)
    step_row = lax.broadcasted_iota(jnp.int32, (q_rows, 16), 0) % n_step
    step_col = lax.broadcasted_iota(jnp.int32, (q_rows, 16), 1)

    def finished_row(f):
        length = lengths[me * (finished + 1) + f]
        owner = owner_of[f]
        rank = slot_of[f] - owner * CAPACITY
        q = jnp.where(
            rank == 0,
            pack_recv[owner, 0:q_rows].astype(F32),
            pack_recv[owner, q_rows:2 * q_rows].astype(F32),
        ).astype(BF16)
        step_k = pack_recv[owner, 2 * q_rows:2 * q_rows + 16]
        step_v = pack_recv[owner, 2 * q_rows + 16:2 * q_rows + 32]
        blks = [table[f, b] for b in range(MAXLEN // block)]
        keys = jnp.concatenate([pool[0, b] for b in blks], axis=0)
        values = jnp.concatenate([pool[1, b] for b in blks], axis=0)
        s = jnp.where(cache_pos < length, dot_nt(q, keys) * SCALE, NEG_FILL)
        seen = (step_col // n_step == rank) & (step_col % n_step <= step_row)
        s2 = jnp.where(seen, dot_nt(q, step_k) * SCALE, NEG_FILL)
        top = jnp.maximum(jnp.max(s, axis=1, keepdims=True), jnp.max(s2, axis=1, keepdims=True))
        p = jnp.exp2(s - top)
        p2 = jnp.exp2(s2 - top)
        norm = jnp.sum(p, axis=1, keepdims=True) + jnp.sum(p2, axis=1, keepdims=True)
        o = dot_nn(p.astype(BF16), values) + dot_nn(p2.astype(BF16), step_v)
        ans[f] = (o / norm).astype(BF16)

    for f in range(finished):
        finished_row(f)

    for n in range(groups * CAPACITY):
        f = jnp.int32(0)
        for j in range(1, finished):
            f = f + jnp.where(slot_of[j] == n, j, 0)
        ans_send[n // CAPACITY, (n % CAPACITY) * q_rows:(n % CAPACITY + 1) * q_rows] = ans[f]

    def send_answer(d, carry):
        peer = (me + d) % groups
        pltpu.make_async_remote_copy(
            src_ref=ans_send.at[peer],
            dst_ref=ans_recv.at[me],
            send_sem=ans_send_sem.at[peer],
            recv_sem=ans_recv_sem.at[me],
            device_id={"group": peer},
            device_id_type=MESH,
        ).start()
        return carry

    lax.fori_loop(1, groups, send_answer, 0)
    ans_recv[me] = ans_send[me]

    q_all = pack_send[:, :CAPACITY * q_rows].reshape(groups * CAPACITY * q_rows, HEAD_DIM)
    n_rows, n_cols = groups * CAPACITY * q_rows, groups * CAPACITY * n_step
    r_id = lax.broadcasted_iota(jnp.int32, (n_rows, n_cols), 0)
    c_id = lax.broadcasted_iota(jnp.int32, (n_rows, n_cols), 1)
    seen_all = (r_id // q_rows == c_id // n_step) & (c_id % n_step <= r_id % n_step)
    s = jnp.where(seen_all, dot_nt(q_all, ks_arr[0]) * SCALE, NEG_FILL)
    p = jnp.exp2(s - jnp.max(s, axis=1, keepdims=True))
    o = dot_nn(p.astype(BF16), ks_arr[1]) / jnp.sum(p, axis=1, keepdims=True)
    step_only[...] = o.astype(BF16).reshape(groups, CAPACITY * q_rows, HEAD_DIM)

    row_id = lax.broadcasted_iota(jnp.int32, (q_rows, res_rows * n_step), 0)
    col_id = lax.broadcasted_iota(jnp.int32, (q_rows, res_rows * n_step), 1)

    def own_rows(r, carry):
        tops, norms = carry
        cols = pl.ds(pl.multiple_of(side * HEAD_DIM, HEAD_DIM), HEAD_DIM)
        q = q_own[r]
        s = dot_nt(q, res[0, r, :, cols])
        s = jnp.where(position < res_len[r], s * SCALE, NEG_FILL)
        seen = (col_id // n_step == r) & (col_id % n_step <= row_id % n_step)
        s2 = jnp.where(seen, dot_nt(q, ks_res[0]) * SCALE, NEG_FILL)
        top = jnp.maximum(jnp.max(s, axis=1, keepdims=True), jnp.max(s2, axis=1, keepdims=True))
        p = jnp.exp2(s - top)
        p2 = jnp.exp2(s2 - top)
        norm = jnp.sum(p, axis=1, keepdims=True) + jnp.sum(p2, axis=1, keepdims=True)
        own_part[r] = dot_nn(p.astype(BF16), res[1, r, :, cols]) + dot_nn(p2.astype(BF16), ks_res[1])
        return jnp.where(lane == r, top, tops), jnp.where(lane == r, norm, norms)

    tops, norms = lax.fori_loop(0, res_rows, own_rows, (zeros, zeros), unroll=4)
    own_stat[0] = tops
    own_stat[1] = norms

    prefill(STACK)
    out_second = pltpu.make_async_copy(
        pout.at[:, pl.ds(half, half)], pout_hbm.at[:, pl.ds(half, half)], out_sem.at[1]
    )
    out_second.start()

    part_pair.wait()
    stat_pair.wait()

    def put_row(dst_row, x):
        for a in range(Q_PER_KV):
            dout[dst_row, :, a * HEAD_DIM:(a + 1) * HEAD_DIM] = x[a * n_step:(a + 1) * n_step].astype(BF16)

    joint = jnp.maximum(own_stat[0], stat_recv[0])
    scale_own = jnp.exp2(own_stat[0] - joint)
    scale_got = jnp.exp2(stat_recv[0] - joint)
    inverse = 1.0 / (own_stat[1] * scale_own + stat_recv[1] * scale_got)
    own_stat[0] = scale_own * inverse
    own_stat[1] = scale_got * inverse

    def merge(r, carry):
        w_own = jnp.sum(jnp.where(lane == r, own_stat[0], 0.0), axis=1, keepdims=True)
        w_got = jnp.sum(jnp.where(lane == r, own_stat[1], 0.0), axis=1, keepdims=True)
        put_row(r, own_part[r] * w_own + part_recv[r].astype(F32) * w_got)
        return carry

    lax.fori_loop(0, res_rows, merge, 0, unroll=4)

    def wait_answer(d, carry):
        peer = (me + d) % groups
        pltpu.make_async_remote_copy(
            src_ref=ans_send.at[peer],
            dst_ref=ans_recv.at[peer],
            send_sem=ans_send_sem.at[peer],
            recv_sem=ans_recv_sem.at[peer],
            device_id={"group": peer},
            device_id_type=MESH,
        ).wait()
        return carry

    lax.fori_loop(1, groups, wait_answer, 0)

    def arrive(src, carry):
        count = jnp.int32(0)
        for f in range(finished):
            count = count + jnp.where(owners[src * finished + f] == me, 1, 0)
        for c in range(CAPACITY):
            rows = slice(c * q_rows, (c + 1) * q_rows)
            x = jnp.where(
                count > c, ans_recv[src, rows].astype(F32), step_only[src, rows].astype(F32)
            )
            put_row(res_rows + src * CAPACITY + c, x)
        return carry

    lax.fori_loop(0, groups, arrive, 0, unroll=2)
    out_dec = pltpu.make_async_copy(dout, dout_hbm, out_sem.at[2])
    out_dec.start()
    out_first.wait()
    out_second.wait()
    out_dec.wait()


def per_device(*args):
    q_prefill, kv_fresh, kv_pool, table, lengths, owners, q_decode, kv_steps, kv_res, res_len = args
    groups = lax.axis_size("group")
    rows, n_step, width = q_decode.shape
    res_rows = kv_res.shape[1]
    arr_rows = rows - res_rows
    q_rows = Q_PER_KV * n_step
    seg = q_prefill.shape[0]
    finished = owners.shape[0] // groups
    vmem = pltpu.VMEM
    scratch = [
        vmem(q_prefill.shape, BF16),
        vmem(kv_fresh.shape, BF16),
        vmem(kv_pool.shape, BF16),
        vmem(q_decode.shape, BF16),
        vmem(kv_steps.shape, BF16),
        vmem(kv_res.shape, BF16),
        vmem(q_prefill.shape, BF16),
        vmem(q_decode.shape, BF16),
        vmem((MAXLEN + seg, HEAD_DIM), BF16),
        vmem((MAXLEN + seg, 2 * HEAD_DIM), BF16),
        vmem((STACK * TILE, TILE), F32),
        vmem((res_rows, q_rows, HEAD_DIM), BF16),
        vmem((res_rows, q_rows, HEAD_DIM), BF16),
        vmem((groups, PACK, HEAD_DIM), BF16),
        vmem((groups, PACK, HEAD_DIM), BF16),
        vmem((2, res_rows * n_step, HEAD_DIM), BF16),
        vmem((2, arr_rows * n_step, HEAD_DIM), BF16),
        vmem((groups, CAPACITY * q_rows, HEAD_DIM), BF16),
        vmem((finished, q_rows, HEAD_DIM), BF16),
        vmem((groups, CAPACITY * q_rows, HEAD_DIM), BF16),
        vmem((groups, CAPACITY * q_rows, HEAD_DIM), BF16),
        vmem((res_rows, q_rows, HEAD_DIM), BF16),
        vmem((res_rows, q_rows, HEAD_DIM), BF16),
        vmem((2, q_rows, HEAD_DIM), F32),
        vmem((2, q_rows, HEAD_DIM), F32),
        vmem((res_rows, q_rows, HEAD_DIM), F32),
        vmem((2, q_rows, HEAD_DIM), F32),
        pltpu.SemaphoreType.DMA((6,)),
        pltpu.SemaphoreType.DMA((3,)),
        pltpu.SemaphoreType.DMA((groups,)),
        pltpu.SemaphoreType.DMA((groups,)),
        pltpu.SemaphoreType.DMA((groups,)),
        pltpu.SemaphoreType.DMA((groups,)),
        pltpu.SemaphoreType.DMA((3,)),
        pltpu.SemaphoreType.DMA((3,)),
    ]
    hbm = pl.BlockSpec(memory_space=pl.ANY)
    smem = pl.BlockSpec(memory_space=pltpu.SMEM)
    return pl.pallas_call(
        functools.partial(kernel, groups),
        out_shape=(
            jax.ShapeDtypeStruct(q_prefill.shape, BF16),
            jax.ShapeDtypeStruct(q_decode.shape, BF16),
        ),
        in_specs=[hbm, hbm, hbm, smem, smem, smem, hbm, hbm, hbm, smem],
        out_specs=(hbm, hbm),
        scratch_shapes=scratch,
        compiler_params=pltpu.CompilerParams(
            collective_id=0, has_side_effects=True, vmem_limit_bytes=56 * 2**20
        ),
        cost_estimate=pl.CostEstimate(
            flops=8 * 10**9, bytes_accessed=21 * 10**6, transcendentals=14 * 10**6
        ),
    )(*args)


def solution(mesh):
    in_specs = (
        P("group", "tp"),
        P(None, "group", "tp"),
        P(None, "group", None, "tp"),
        P("group", None),
        P(),
        P(),
        P("group", None, "tp"),
        P(None, "group", None, "tp"),
        P(None, "group", "tp", None),
        P("group"),
    )
    out_specs = (P("group", "tp"), P("group", None, "tp"))
    return jax.shard_map(
        per_device, mesh=mesh, in_specs=in_specs, out_specs=out_specs, check_vma=False
    )
```

time: 523 us -> 58.5 us (0.11)
  waiting for transfers between devices: 257 us -> 0 us
  other arithmetic: 84.4 us -> 0 us
  local copies, waits for them, and re-layouts: 88.1 us -> 3.93 us
  matrix products: 74.1 us -> 0 us
  Pallas kernels: 0 us -> 53.7 us
  starting transfers between devices: 15 us -> 0 us
    all_to_all x1 -> x0, waiting for transfers between devices: 174 us -> none  [per_device(): lax.all_to_all(picked.reshape(2, groups, CAPACITY, fin_data.shape[2], fin...]
    ppermute x5 -> x0, waiting for transfers between devices: 83 us -> none  [swapped(): lax.ppermute(x, axis, [(i, i ^ 1 << stride) for i in range(lax.axis_size(...]
    dot_general x22 -> x0, matrix products: 74.1 us -> none  [the longest x8 29.9 us: one_head(): jnp.einsum('id,ld->il', query_rows, kv_pair[0], preferred_element_type=jn...]
    pallas_call x0 -> x1, Pallas kernels: none -> 53.7 us  [per_device(): pl.pallas_call(functools.partial(kernel, groups), out_shape=(jax.ShapeDty...]
    select_n x7 -> x0, other arithmetic: 47.1 us -> none  [the longest x2 19.9 us: pair_join(): jnp.where(pair_side == 0, jnp.concatenate([own_part, other_part], axis=-1...]
    reduce_sum x14 -> x0, other arithmetic: 33.6 us -> none  [the longest x8 28 us: one_head(): normalizer = jnp.sum(expo_vals, axis=-1)]
    gather x5 -> x0, local copies, waits for them, and re-layouts: 32.6 us -> none  [the longest x2 18.3 us: per_device(): kv_pool[:, block_table[:finished]].reshape(2, finished, MAXLEN, width_own)]
    all_to_all x1 -> x0, local copies, waits for them, and re-layouts: 22.4 us -> none  [per_device(): lax.all_to_all(picked.reshape(2, groups, CAPACITY, fin_data.shape[2], fin...]
  transfers between devices with their start and end apart: 6 -> 0, of which waited for: 3 -> 0; matrix products, arithmetic and copies ran while one was open for 33% -> 0% of each run, Pallas kernels for 0% -> 0%
where the time goes in v1:
time: 58.5 us; the launch traced here: 58.3 us
  Pallas kernels  53.7 us (92%)
  local copies, waits for them, and re-layouts  3.93 us (7%)
  between operations  0.65 us (1%)
    pallas_call x1, Pallas kernels, per_device(): pl.pallas_call(functools.partial(kernel, groups), out_shape=(jax.ShapeDty...  53.7 us
    unnamed x4, local copies, waits for them, and re-layouts  3.93 us

profile of v1, /device:TPU:1, one launch (start us, length us, event | category | flops | bytes accessed | tf_op | source)
XLA Modules:
  0.0 58.3 jit_solution(570332519727625722)
XLA Ops:
  0.6 53.7 %shard_map.113 = (bf16[1024,1024]{1,0:T(8,128)(2,1)}, bf16[64,4,1024]{2,1,0:T(4,128)(2,1)}) custom-call(bf16[1024,1024]{1,0:T(8,128)(2,1)} %qp_hbm.1, bf16[2,1024,128]{2,1,0:T(8,128)(2,1)} %fresh_hbm.1, bf16[2,208,64,128]{3,2,1,0:T(8,128)(2,1)} %pool_hbm.1, s32[13,16]{1,0:T(8,128)} %table.1, s32[208]{0:T(256)} %lengths.1, s32[192]{0:T(256)} %owners.1, ...), custom_call_target="tpu_custom_call" | custom-call | flops 8000000000 | bytes 21000000 | tf_op jit(solution)/shard_map/pallas_call | solution.py:475
  54.3 0.0 copy-start
  54.4 3.1 %copy.14 = bf16[1024,1024]{1,0:T(8,128)(2,1)} copy(bf16[1024,1024]{1,0:T(8,128)(2,1)} %get-tuple-element.4) | data formatting | bytes 4194304
  57.5 0.0 copy-done
  57.5 0.8 %copy.15 = bf16[64,4,1024]{2,1,0:T(4,128)(2,1)} copy(bf16[64,4,1024]{2,1,0:T(4,128)(2,1)S(1)} %copy-done) | data formatting | bytes 1048576
Async XLA Ops:
  54.3 3.1 %copy-start = (bf16[64,4,1024]{2,1,0:T(4,128)(2,1)S(1)}, bf16[64,4,1024]{2,1,0:T(4,128)(2,1)}, u32[]{:S(2)}) copy-start(bf16[64,4,1024]{2,1,0:T(4,128)(2,1)} %get-tuple-element.5) | copy-start | bytes 1572868

commit v2 on v1

--- a/solution.py
+++ b/solution.py
@@ -15,7 +15,9 @@
 SCALE = HEAD_DIM ** -0.5 * 1.4426950408889634
 PACK = 96
 TILE = 128
-STACK = 4
+STACK = 8
+BATCH = 8
+FIN_BATCH = 4
 MESH = pl.DeviceIdType.MESH
 BF16 = jnp.bfloat16
 F32 = jnp.float32
@@ -60,12 +62,13 @@
     kbuf,
     vbuf,
     diag,
-    q_own,
-    q_partner,
+    q_pair,
     pack_send,
     pack_recv,
     ks_res,
     ks_arr,
+    step_part,
+    step_stat,
     step_only,
     ans,
     ans_send,
@@ -122,7 +125,7 @@
     loads[1].wait()
 
     def relay_res(r, carry):
-        q_own[r] = heads_to_rows(qd[r])
+        q_pair[side, r] = heads_to_rows(qd[r])
         return carry
 
     lax.fori_loop(0, res_rows, relay_res, 0, unroll=4)
@@ -139,38 +142,6 @@
         return carry
 
     lax.fori_loop(0, groups, relay_arr, 0, unroll=2)
-
-    pl.semaphore_wait(barrier, groups)
-
-    def pack_copy(peer):
-        return pltpu.make_async_remote_copy(
-            src_ref=pack_send.at[peer],
-            dst_ref=pack_recv.at[me],
-            send_sem=pack_send_sem.at[peer],
-            recv_sem=pack_recv_sem.at[me],
-            device_id={"group": peer},
-            device_id_type=MESH,
-        )
-
-    def pair_copy(src, dst, i):
-        return pltpu.make_async_remote_copy(
-            src_ref=src,
-            dst_ref=dst,
-            send_sem=pair_send_sem.at[i],
-            recv_sem=pair_recv_sem.at[i],
-            device_id={"tp": partner},
-            device_id_type=MESH,
-        )
-
-    q_pair = pair_copy(q_own, q_partner, 0)
-    q_pair.start()
-
-    def send_pack(d, carry):
-        pack_copy((me + d) % groups).start()
-        return carry
-
-    lax.fori_loop(1, groups, send_pack, 0)
-    pack_recv[me] = pack_send[me]
 
     per_tile = 16 // n_step
 
@@ -208,49 +179,110 @@
     diag[...] = jnp.where(col <= row, 0.0, NEG_FILL)
     loads[4].wait()
 
-    def prefill(first_head):
-        cols = [slice((first_head + h) * HEAD_DIM, (first_head + h + 1) * HEAD_DIM) for h in range(STACK)]
-        for i in range(seg // TILE):
-            rows = slice(i * TILE, (i + 1) * TILE)
-            span = MAXLEN + (i + 1) * TILE
-            q = jnp.concatenate([qp[rows, c] for c in cols], axis=0)
-            s = dot_nt(q, kbuf[:span])
-            s = jnp.concatenate([s[:, :span - TILE], s[:, span - TILE:] + diag[...]], axis=1)
-            top = jnp.max(s, axis=1, keepdims=True)
-            p = jnp.exp2(s * SCALE - top * SCALE).astype(BF16)
-            o = dot_nn(p, vbuf[:span])
-            o = (o[:, :HEAD_DIM] / o[:, HEAD_DIM:]).astype(BF16)
-            for h in range(STACK):
-                pout[rows, cols[h]] = o[h * TILE:(h + 1) * TILE]
+    def prefill(i):
+        rows = slice(i * TILE, (i + 1) * TILE)
+        span = MAXLEN + (i + 1) * TILE
+        cols = [slice(h * HEAD_DIM, (h + 1) * HEAD_DIM) for h in range(STACK)]
+        q = jnp.concatenate([qp[rows, c] for c in cols], axis=0)
+        s = dot_nt(q, kbuf[:span])
+        s = jnp.concatenate([s[:, :span - TILE], s[:, span - TILE:] + diag[...]], axis=1)
+        top = jnp.max(s, axis=1, keepdims=True)
+        p = jnp.exp2(s * SCALE - top * SCALE).astype(BF16)
+        o = dot_nn(p, vbuf[:span])
+        o = (o[:, :HEAD_DIM] / o[:, HEAD_DIM:]).astype(BF16)
+        for h in range(STACK):
+            pout[rows, cols[h]] = o[h * TILE:(h + 1) * TILE]
+
+    def out_rows(first, last, i):
+        rows = pl.ds(first * TILE, (last - first) * TILE)
+        copy = pltpu.make_async_copy(pout.at[rows], pout_hbm.at[rows], out_sem.at[i])
+        copy.start()
+        return copy
 
     prefill(0)
-    half = STACK * HEAD_DIM
-    out_first = pltpu.make_async_copy(
-        pout.at[:, pl.ds(0, half)], pout_hbm.at[:, pl.ds(0, half)], out_sem.at[0]
-    )
-    out_first.start()
+
+    pl.semaphore_wait(barrier, groups)
+
+    def pack_copy(peer):
+        return pltpu.make_async_remote_copy(
+            src_ref=pack_send.at[peer],
+            dst_ref=pack_recv.at[me],
+            send_sem=pack_send_sem.at[peer],
+            recv_sem=pack_recv_sem.at[me],
+            device_id={"group": peer},
+            device_id_type=MESH,
+        )
+
+    def pair_copy(src, dst, i):
+        return pltpu.make_async_remote_copy(
+            src_ref=src,
+            dst_ref=dst,
+            send_sem=pair_send_sem.at[i],
+            recv_sem=pair_recv_sem.at[i],
+            device_id={"tp": partner},
+            device_id_type=MESH,
+        )
+
+    q_copy = pair_copy(q_pair.at[side], q_pair.at[side], 0)
+    q_copy.start()
+
+    def send_pack(d, carry):
+        pack_copy((me + d) % groups).start()
+        return carry
+
+    lax.fori_loop(1, groups, send_pack, 0)
+    pack_recv[me] = pack_send[me]
+
+
+    for i in range(1, 5):
+        prefill(i)
+    out_first = out_rows(0, 5, 0)
 
     loads[5].wait()
-    q_pair.wait()
+    q_copy.wait()
     lane = lax.broadcasted_iota(jnp.int32, (q_rows, HEAD_DIM), 1)
-    position = side * span_res + lax.broadcasted_iota(jnp.int32, (q_rows, span_res), 1)
-
-    def partner_rows(r, carry):
+    position = side * span_res + lax.broadcasted_iota(jnp.int32, (2 * q_rows, span_res), 1)
+    empty = jnp.zeros((q_rows, HEAD_DIM), BF16)
+
+    def resident_rows(i, carry):
         tops, norms = carry
-        cols = pl.ds(pl.multiple_of((1 - side) * HEAD_DIM, HEAD_DIM), HEAD_DIM)
-        s = dot_nt(q_partner[r], res[0, r, :, cols])
-        s = jnp.where(position < res_len[r], s * SCALE, NEG_FILL)
-        top = jnp.max(s, axis=1, keepdims=True)
-        p = jnp.exp2(s - top)
-        norm = jnp.sum(p, axis=1, keepdims=True)
-        part_send[r] = dot_nn(p.astype(BF16), res[1, r, :, cols]).astype(BF16)
-        return jnp.where(lane == r, top, tops), jnp.where(lane == r, norm, norms)
+        rows = [i * BATCH + b for b in range(BATCH)]
+        scores = []
+        for r in rows:
+            q = jnp.concatenate(
+                [
+                    jnp.concatenate([q_pair[0, r], empty], axis=1),
+                    jnp.concatenate([empty, q_pair[1, r]], axis=1),
+                ],
+                axis=0,
+            )
+            scores.append(dot_nt(q, res[0, r]))
+        scores = [
+            jnp.where(position < res_len[r], s * SCALE, NEG_FILL) for r, s in zip(rows, scores)
+        ]
+        maxima = [jnp.max(s, axis=1, keepdims=True) for s in scores]
+        weights = [jnp.exp2(s - m) for s, m in zip(scores, maxima)]
+        sums = [jnp.sum(p, axis=1, keepdims=True) for p in weights]
+        outs = [dot_nn(p.astype(BF16), res[1, r]) for r, p in zip(rows, weights)]
+        for r, m, l, o in zip(rows, maxima, sums, outs):
+            for u in range(2):
+                head = slice(u * q_rows, (u + 1) * q_rows)
+                part = o[head, u * HEAD_DIM:(u + 1) * HEAD_DIM]
+                own_part[u, r] = part
+                part_send[u, r] = part.astype(BF16)
+                own_stat[0, u, r] = jnp.broadcast_to(m[head], (q_rows, HEAD_DIM))
+                own_stat[1, u, r] = jnp.broadcast_to(l[head], (q_rows, HEAD_DIM))
+            give = jnp.where(side == 0, m[q_rows:], m[:q_rows])
+            tops = jnp.where(lane == r, give, tops)
+            give = jnp.where(side == 0, l[q_rows:], l[:q_rows])
+            norms = jnp.where(lane == r, give, norms)
+        return tops, norms
 
     zeros = jnp.zeros((q_rows, HEAD_DIM), F32)
-    tops, norms = lax.fori_loop(0, res_rows, partner_rows, (zeros, zeros), unroll=4)
+    tops, norms = lax.fori_loop(0, res_rows // BATCH, resident_rows, (zeros, zeros))
     stat_send[0] = tops
     stat_send[1] = norms
-    part_pair = pair_copy(part_send, part_recv, 1)
+    part_pair = pair_copy(part_send.at[1 - side], part_recv, 1)
     part_pair.start()
     stat_pair = pair_copy(stat_send, stat_recv, 2)
     stat_pair.start()
@@ -281,32 +313,40 @@
     step_row = lax.broadcasted_iota(jnp.int32, (q_rows, 16), 0) % n_step
     step_col = lax.broadcasted_iota(jnp.int32, (q_rows, 16), 1)
 
-    def finished_row(f):
-        length = lengths[me * (finished + 1) + f]
-        owner = owner_of[f]
-        rank = slot_of[f] - owner * CAPACITY
-        q = jnp.where(
-            rank == 0,
-            pack_recv[owner, 0:q_rows].astype(F32),
-            pack_recv[owner, q_rows:2 * q_rows].astype(F32),
-        ).astype(BF16)
-        step_k = pack_recv[owner, 2 * q_rows:2 * q_rows + 16]
-        step_v = pack_recv[owner, 2 * q_rows + 16:2 * q_rows + 32]
-        blks = [table[f, b] for b in range(MAXLEN // block)]
-        keys = jnp.concatenate([pool[0, b] for b in blks], axis=0)
-        values = jnp.concatenate([pool[1, b] for b in blks], axis=0)
-        s = jnp.where(cache_pos < length, dot_nt(q, keys) * SCALE, NEG_FILL)
-        seen = (step_col // n_step == rank) & (step_col % n_step <= step_row)
-        s2 = jnp.where(seen, dot_nt(q, step_k) * SCALE, NEG_FILL)
-        top = jnp.maximum(jnp.max(s, axis=1, keepdims=True), jnp.max(s2, axis=1, keepdims=True))
-        p = jnp.exp2(s - top)
-        p2 = jnp.exp2(s2 - top)
-        norm = jnp.sum(p, axis=1, keepdims=True) + jnp.sum(p2, axis=1, keepdims=True)
-        o = dot_nn(p.astype(BF16), values) + dot_nn(p2.astype(BF16), step_v)
-        ans[f] = (o / norm).astype(BF16)
-
-    for f in range(finished):
-        finished_row(f)
+    def finished_rows(batch):
+        scores, step_scores, step_values = [], [], []
+        for f in batch:
+            owner = owner_of[f]
+            rank = slot_of[f] - owner * CAPACITY
+            q = jnp.where(
+                rank == 0,
+                pack_recv[owner, 0:q_rows].astype(F32),
+                pack_recv[owner, q_rows:2 * q_rows].astype(F32),
+            ).astype(BF16)
+            keys = jnp.concatenate([pool[0, table[f, b]] for b in range(MAXLEN // block)], axis=0)
+            length = lengths[me * (finished + 1) + f]
+            scores.append(jnp.where(cache_pos < length, dot_nt(q, keys) * SCALE, NEG_FILL))
+            seen = (step_col // n_step == rank) & (step_col % n_step <= step_row)
+            step_k = pack_recv[owner, 2 * q_rows:2 * q_rows + 16]
+            step_scores.append(jnp.where(seen, dot_nt(q, step_k) * SCALE, NEG_FILL))
+            step_values.append(pack_recv[owner, 2 * q_rows + 16:2 * q_rows + 32])
+        maxima = [
+            jnp.maximum(jnp.max(s, axis=1, keepdims=True), jnp.max(s2, axis=1, keepdims=True))
+            for s, s2 in zip(scores, step_scores)
+        ]
+        weights = [jnp.exp2(s - m) for s, m in zip(scores, maxima)]
+        step_weights = [jnp.exp2(s - m) for s, m in zip(step_scores, maxima)]
+        sums = [
+            jnp.sum(p, axis=1, keepdims=True) + jnp.sum(p2, axis=1, keepdims=True)
+            for p, p2 in zip(weights, step_weights)
+        ]
+        for f, p, p2, v2, l in zip(batch, weights, step_weights, step_values, sums):
+            values = jnp.concatenate([pool[1, table[f, b]] for b in range(MAXLEN // block)], axis=0)
+            o = dot_nn(p.astype(BF16), values) + dot_nn(p2.astype(BF16), v2)
+            ans[f] = (o / l).astype(BF16)
+
+    for first in range(0, finished, FIN_BATCH):
+        finished_rows(range(first, min(first + FIN_BATCH, finished)))
 
     for n in range(groups * CAPACITY):
         f = jnp.int32(0)
@@ -329,43 +369,31 @@
     lax.fori_loop(1, groups, send_answer, 0)
     ans_recv[me] = ans_send[me]
 
-    q_all = pack_send[:, :CAPACITY * q_rows].reshape(groups * CAPACITY * q_rows, HEAD_DIM)
-    n_rows, n_cols = groups * CAPACITY * q_rows, groups * CAPACITY * n_step
+
+    n_rows, n_cols = res_rows * q_rows, res_rows * n_step
     r_id = lax.broadcasted_iota(jnp.int32, (n_rows, n_cols), 0)
     c_id = lax.broadcasted_iota(jnp.int32, (n_rows, n_cols), 1)
     seen_all = (r_id // q_rows == c_id // n_step) & (c_id % n_step <= r_id % n_step)
-    s = jnp.where(seen_all, dot_nt(q_all, ks_arr[0]) * SCALE, NEG_FILL)
-    p = jnp.exp2(s - jnp.max(s, axis=1, keepdims=True))
-    o = dot_nn(p.astype(BF16), ks_arr[1]) / jnp.sum(p, axis=1, keepdims=True)
-    step_only[...] = o.astype(BF16).reshape(groups, CAPACITY * q_rows, HEAD_DIM)
-
-    row_id = lax.broadcasted_iota(jnp.int32, (q_rows, res_rows * n_step), 0)
-    col_id = lax.broadcasted_iota(jnp.int32, (q_rows, res_rows * n_step), 1)
-
-    def own_rows(r, carry):
-        tops, norms = carry
-        cols = pl.ds(pl.multiple_of(side * HEAD_DIM, HEAD_DIM), HEAD_DIM)
-        q = q_own[r]
-        s = dot_nt(q, res[0, r, :, cols])
-        s = jnp.where(position < res_len[r], s * SCALE, NEG_FILL)
-        seen = (col_id // n_step == r) & (col_id % n_step <= row_id % n_step)
-        s2 = jnp.where(seen, dot_nt(q, ks_res[0]) * SCALE, NEG_FILL)
-        top = jnp.maximum(jnp.max(s, axis=1, keepdims=True), jnp.max(s2, axis=1, keepdims=True))
+
+    def all_steps(q, keys, values):
+        s = jnp.where(seen_all, dot_nt(q, keys) * SCALE, NEG_FILL)
+        top = jnp.max(s, axis=1, keepdims=True)
         p = jnp.exp2(s - top)
-        p2 = jnp.exp2(s2 - top)
-        norm = jnp.sum(p, axis=1, keepdims=True) + jnp.sum(p2, axis=1, keepdims=True)
-        own_part[r] = dot_nn(p.astype(BF16), res[1, r, :, cols]) + dot_nn(p2.astype(BF16), ks_res[1])
-        return jnp.where(lane == r, top, tops), jnp.where(lane == r, norm, norms)
-
-    tops, norms = lax.fori_loop(0, res_rows, own_rows, (zeros, zeros), unroll=4)
-    own_stat[0] = tops
-    own_stat[1] = norms
-
-    prefill(STACK)
-    out_second = pltpu.make_async_copy(
-        pout.at[:, pl.ds(half, half)], pout_hbm.at[:, pl.ds(half, half)], out_sem.at[1]
-    )
-    out_second.start()
+        return dot_nn(p.astype(BF16), values), top, jnp.sum(p, axis=1, keepdims=True)
+
+    q_arr = pack_send[:, :CAPACITY * q_rows].reshape(n_rows, HEAD_DIM)
+    o, top, norm = all_steps(q_arr, ks_arr[0], ks_arr[1])
+    step_only[...] = (o / norm).astype(BF16).reshape(groups, CAPACITY * q_rows, HEAD_DIM)
+    q_res = q_pair[side].reshape(n_rows, HEAD_DIM)
+    o, top, norm = all_steps(q_res, ks_res[0], ks_res[1])
+    rows3 = (res_rows, q_rows, HEAD_DIM)
+    step_part[...] = o.reshape(rows3)
+    step_stat[0] = jnp.broadcast_to(top, o.shape).reshape(rows3)
+    step_stat[1] = jnp.broadcast_to(norm, o.shape).reshape(rows3)
+
+    for i in range(5, 8):
+        prefill(i)
+    out_second = out_rows(5, 8, 1)
 
     part_pair.wait()
     stat_pair.wait()
@@ -374,17 +402,17 @@
         for a in range(Q_PER_KV):
             dout[dst_row, :, a * HEAD_DIM:(a + 1) * HEAD_DIM] = x[a * n_step:(a + 1) * n_step].astype(BF16)
 
-    joint = jnp.maximum(own_stat[0], stat_recv[0])
-    scale_own = jnp.exp2(own_stat[0] - joint)
-    scale_got = jnp.exp2(stat_recv[0] - joint)
-    inverse = 1.0 / (own_stat[1] * scale_own + stat_recv[1] * scale_got)
-    own_stat[0] = scale_own * inverse
-    own_stat[1] = scale_got * inverse
-
     def merge(r, carry):
-        w_own = jnp.sum(jnp.where(lane == r, own_stat[0], 0.0), axis=1, keepdims=True)
-        w_got = jnp.sum(jnp.where(lane == r, own_stat[1], 0.0), axis=1, keepdims=True)
-        put_row(r, own_part[r] * w_own + part_recv[r].astype(F32) * w_got)
+        top_own, top_step = own_stat[0, side, r], step_stat[0, r]
+        top_got = jnp.sum(jnp.where(lane == r, stat_recv[0], 0.0), axis=1, keepdims=True)
+        norm_got = jnp.sum(jnp.where(lane == r, stat_recv[1], 0.0), axis=1, keepdims=True)
+        joint = jnp.maximum(jnp.maximum(top_own, top_step), top_got)
+        w_own = jnp.exp2(top_own - joint)
+        w_step = jnp.exp2(top_step - joint)
+        w_got = jnp.exp2(top_got - joint)
+        norm = own_stat[1, side, r] * w_own + step_stat[1, r] * w_step + norm_got * w_got
+        x = own_part[side, r] * w_own + step_part[r] * w_step + part_recv[r].astype(F32) * w_got
+        put_row(r, x / norm)
         return carry
 
     lax.fori_loop(0, res_rows, merge, 0, unroll=4)
@@ -445,22 +473,23 @@
         vmem((MAXLEN + seg, HEAD_DIM), BF16),
         vmem((MAXLEN + seg, 2 * HEAD_DIM), BF16),
         vmem((STACK * TILE, TILE), F32),
-        vmem((res_rows, q_rows, HEAD_DIM), BF16),
-        vmem((res_rows, q_rows, HEAD_DIM), BF16),
+        vmem((2, res_rows, q_rows, HEAD_DIM), BF16),
         vmem((groups, PACK, HEAD_DIM), BF16),
         vmem((groups, PACK, HEAD_DIM), BF16),
         vmem((2, res_rows * n_step, HEAD_DIM), BF16),
         vmem((2, arr_rows * n_step, HEAD_DIM), BF16),
+        vmem((res_rows, q_rows, HEAD_DIM), F32),
+        vmem((2, res_rows, q_rows, HEAD_DIM), F32),
         vmem((groups, CAPACITY * q_rows, HEAD_DIM), BF16),
         vmem((finished, q_rows, HEAD_DIM), BF16),
         vmem((groups, CAPACITY * q_rows, HEAD_DIM), BF16),
         vmem((groups, CAPACITY * q_rows, HEAD_DIM), BF16),
-        vmem((res_rows, q_rows, HEAD_DIM), BF16),
+        vmem((2, res_rows, q_rows, HEAD_DIM), BF16),
         vmem((res_rows, q_rows, HEAD_DIM), BF16),
         vmem((2, q_rows, HEAD_DIM), F32),
         vmem((2, q_rows, HEAD_DIM), F32),
-        vmem((res_rows, q_rows, HEAD_DIM), F32),
-        vmem((2, q_rows, HEAD_DIM), F32),
+        vmem((2, res_rows, q_rows, HEAD_DIM), F32),
+        vmem((2, 2, res_rows, q_rows, HEAD_DIM), F32),
         pltpu.SemaphoreType.DMA((6,)),
         pltpu.SemaphoreType.DMA((3,)),
         pltpu.SemaphoreType.DMA((groups,)),

time: 58.5 us -> 41 us (0.70)
  Pallas kernels: 53.7 us -> 36.2 us
    pallas_call x1, Pallas kernels: 53.7 us -> 36.2 us  [per_device(): pl.pallas_call(functools.partial(kernel, groups), out_shape=(jax.ShapeDty...]
where the time goes in v2:
time: 41 us; the launch traced here: 40.8 us
  Pallas kernels  36.2 us (88%)
  local copies, waits for them, and re-layouts  3.93 us (10%)
  between operations  0.65 us (2%)
    pallas_call x1, Pallas kernels, per_device(): pl.pallas_call(functools.partial(kernel, groups), out_shape=(jax.ShapeDty...  36.2 us
    unnamed x4, local copies, waits for them, and re-layouts  3.93 us

profile of v2, /device:TPU:1, one launch (start us, length us, event | category | flops | bytes accessed | tf_op | source)
XLA Modules:
  0.0 40.8 jit_solution(7100140569082786942)
XLA Ops:
  0.6 36.2 %shard_map.113 = (bf16[1024,1024]{1,0:T(8,128)(2,1)}, bf16[64,4,1024]{2,1,0:T(4,128)(2,1)}) custom-call(bf16[1024,1024]{1,0:T(8,128)(2,1)} %qp_hbm.1, bf16[2,1024,128]{2,1,0:T(8,128)(2,1)} %fresh_hbm.1, bf16[2,208,64,128]{3,2,1,0:T(8,128)(2,1)} %pool_hbm.1, s32[13,16]{1,0:T(8,128)} %table.1, s32[208]{0:T(256)} %lengths.1, s32[192]{0:T(256)} %owners.1, ...), custom_call_target="tpu_custom_call" | custom-call | flops 8000000000 | bytes 21000000 | tf_op jit(solution)/shard_map/pallas_call | solution.py:504
  36.9 0.0 copy-start
  36.9 3.1 %copy.14 = bf16[1024,1024]{1,0:T(8,128)(2,1)} copy(bf16[1024,1024]{1,0:T(8,128)(2,1)} %get-tuple-element.4) | data formatting | bytes 4194304
  40.0 0.0 copy-done
  40.0 0.8 %copy.15 = bf16[64,4,1024]{2,1,0:T(4,128)(2,1)} copy(bf16[64,4,1024]{2,1,0:T(4,128)(2,1)S(1)} %copy-done) | data formatting | bytes 1048576
Async XLA Ops:
  36.9 3.1 %copy-start = (bf16[64,4,1024]{2,1,0:T(4,128)(2,1)S(1)}, bf16[64,4,1024]{2,1,0:T(4,128)(2,1)}, u32[]{:S(2)}) copy-start(bf16[64,4,1024]{2,1,0:T(4,128)(2,1)} %get-tuple-element.5) | copy-start | bytes 1572868

commit v3 on v2

--- a/solution.py
+++ b/solution.py
@@ -118,7 +118,7 @@
         pltpu.make_async_copy(qp_hbm, qp, load_sem.at[4]),
         pltpu.make_async_copy(res_hbm, res, load_sem.at[5]),
     ]
-    for one in loads:
+    for one in loads[:5]:
         one.start()
 
     loads[0].wait()
@@ -143,6 +143,39 @@
 
     lax.fori_loop(0, groups, relay_arr, 0, unroll=2)
 
+    pl.semaphore_wait(barrier, groups)
+
+    def pack_copy(peer):
+        return pltpu.make_async_remote_copy(
+            src_ref=pack_send.at[peer],
+            dst_ref=pack_recv.at[me],
+            send_sem=pack_send_sem.at[peer],
+            recv_sem=pack_recv_sem.at[me],
+            device_id={"group": peer},
+            device_id_type=MESH,
+        )
+
+    def pair_copy(src, dst, i):
+        return pltpu.make_async_remote_copy(
+            src_ref=src,
+            dst_ref=dst,
+            send_sem=pair_send_sem.at[i],
+            recv_sem=pair_recv_sem.at[i],
+            device_id={"tp": partner},
+            device_id_type=MESH,
+        )
+
+    q_copy = pair_copy(q_pair.at[side], q_pair.at[side], 0)
+    q_copy.start()
+
+    def send_pack(d, carry):
+        pack_copy((me + d) % groups).start()
+        return carry
+
+    lax.fori_loop(1, groups, send_pack, 0)
+    pack_recv[me] = pack_send[me]
+
+
     per_tile = 16 // n_step
 
     def gather_steps(i, carry):
@@ -158,6 +191,7 @@
 
     loads[2].wait()
     loads[3].wait()
+    loads[5].start()
     ctx_len = lengths[me * (finished + 1) + finished]
     first_key = pool[0, table[finished, 0]][0:1]
     block = pool.shape[2]
@@ -199,42 +233,7 @@
         copy.start()
         return copy
 
-    prefill(0)
-
-    pl.semaphore_wait(barrier, groups)
-
-    def pack_copy(peer):
-        return pltpu.make_async_remote_copy(
-            src_ref=pack_send.at[peer],
-            dst_ref=pack_recv.at[me],
-            send_sem=pack_send_sem.at[peer],
-            recv_sem=pack_recv_sem.at[me],
-            device_id={"group": peer},
-            device_id_type=MESH,
-        )
-
-    def pair_copy(src, dst, i):
-        return pltpu.make_async_remote_copy(
-            src_ref=src,
-            dst_ref=dst,
-            send_sem=pair_send_sem.at[i],
-            recv_sem=pair_recv_sem.at[i],
-            device_id={"tp": partner},
-            device_id_type=MESH,
-        )
-
-    q_copy = pair_copy(q_pair.at[side], q_pair.at[side], 0)
-    q_copy.start()
-
-    def send_pack(d, carry):
-        pack_copy((me + d) % groups).start()
-        return carry
-
-    lax.fori_loop(1, groups, send_pack, 0)
-    pack_recv[me] = pack_send[me]
-
-
-    for i in range(1, 5):
+    for i in range(5):
         prefill(i)
     out_first = out_rows(0, 5, 0)
 

time: 41 us -> 43.2 us (1.054)
  Pallas kernels: 36.2 us -> 38.4 us
    pallas_call x1, Pallas kernels: 36.2 us -> 38.4 us  [per_device(): pl.pallas_call(functools.partial(kernel, groups), out_shape=(jax.ShapeDty...]
where the time goes in v3:
time: 43.2 us; the launch traced here: 43 us
  Pallas kernels  38.4 us (89%)
  local copies, waits for them, and re-layouts  3.93 us (9%)
  between operations  0.65 us (2%)
    pallas_call x1, Pallas kernels, per_device(): pl.pallas_call(functools.partial(kernel, groups), out_shape=(jax.ShapeDty...  38.4 us
    unnamed x4, local copies, waits for them, and re-layouts  3.93 us

profile of v3, /device:TPU:1, one launch (start us, length us, event | category | flops | bytes accessed | tf_op | source)
XLA Modules:
  0.0 43.0 jit_solution(13116735483464418585)
XLA Ops:
  0.6 38.4 %shard_map.113 = (bf16[1024,1024]{1,0:T(8,128)(2,1)}, bf16[64,4,1024]{2,1,0:T(4,128)(2,1)}) custom-call(bf16[1024,1024]{1,0:T(8,128)(2,1)} %qp_hbm.1, bf16[2,1024,128]{2,1,0:T(8,128)(2,1)} %fresh_hbm.1, bf16[2,208,64,128]{3,2,1,0:T(8,128)(2,1)} %pool_hbm.1, s32[13,16]{1,0:T(8,128)} %table.1, s32[208]{0:T(256)} %lengths.1, s32[192]{0:T(256)} %owners.1, ...), custom_call_target="tpu_custom_call" | custom-call | flops 8000000000 | bytes 21000000 | tf_op jit(solution)/shard_map/pallas_call | solution.py:503
  39.0 0.0 copy-start
  39.1 3.1 %copy.14 = bf16[1024,1024]{1,0:T(8,128)(2,1)} copy(bf16[1024,1024]{1,0:T(8,128)(2,1)} %get-tuple-element.4) | data formatting | bytes 4194304
  42.2 0.0 copy-done
  42.2 0.8 %copy.15 = bf16[64,4,1024]{2,1,0:T(4,128)(2,1)} copy(bf16[64,4,1024]{2,1,0:T(4,128)(2,1)S(1)} %copy-done) | data formatting | bytes 1048576
Async XLA Ops:
  39.0 3.1 %copy-start = (bf16[64,4,1024]{2,1,0:T(4,128)(2,1)S(1)}, bf16[64,4,1024]{2,1,0:T(4,128)(2,1)}, u32[]{:S(2)}) copy-start(bf16[64,4,1024]{2,1,0:T(4,128)(2,1)} %get-tuple-element.5) | copy-start | bytes 1572868

commit v4 on v2

--- a/solution.py
+++ b/solution.py
@@ -18,6 +18,9 @@
 STACK = 8
 BATCH = 8
 FIN_BATCH = 4
+EARLY = 2
+MIDDLE = 5
+LAST = 7
 MESH = pl.DeviceIdType.MESH
 BF16 = jnp.bfloat16
 F32 = jnp.float32
@@ -35,6 +38,48 @@
     wide = x.astype(F32)
     parts = [wide[:, a * HEAD_DIM:(a + 1) * HEAD_DIM] for a in range(Q_PER_KV)]
     return jnp.concatenate(parts, axis=0).astype(BF16)
+
+
+def prefill_block(q_cols, kbuf, vbuf, diag, span):
+    q = jnp.concatenate(
+        [q_cols[:, h * HEAD_DIM:(h + 1) * HEAD_DIM] for h in range(STACK)], axis=0
+    )
+    s = dot_nt(q, kbuf[:span])
+    s = jnp.concatenate([s[:, :span - TILE], s[:, span - TILE:] + diag[...]], axis=1)
+    top = jnp.max(s, axis=1, keepdims=True)
+    p = jnp.exp2(s * SCALE - top * SCALE).astype(BF16)
+    o = dot_nn(p, vbuf[:span])
+    return (o[:, :HEAD_DIM] / o[:, HEAD_DIM:]).astype(BF16)
+
+
+def fill_diag(diag):
+    row = lax.broadcasted_iota(jnp.int32, (STACK * TILE, TILE), 0) % TILE
+    col = lax.broadcasted_iota(jnp.int32, (STACK * TILE, TILE), 1)
+    diag[...] = jnp.where(col <= row, 0.0, NEG_FILL)
+
+
+def tail_kernel(qp_hbm, k_hbm, v_hbm, part_hbm, dec_hbm, pout_hbm, dout_hbm, qp, kbuf, vbuf, out, diag, sem):
+    done = part_hbm.shape[0]
+    rest = pl.ds(done, pout_hbm.shape[0] - done)
+    load_q = pltpu.make_async_copy(qp_hbm.at[rest], qp, sem.at[0])
+    load_k = pltpu.make_async_copy(k_hbm, kbuf, sem.at[1])
+    load_v = pltpu.make_async_copy(v_hbm, vbuf, sem.at[2])
+    move_dec = pltpu.make_async_copy(dec_hbm, dout_hbm, sem.at[3])
+    move_part = pltpu.make_async_copy(part_hbm, pout_hbm.at[pl.ds(0, done)], sem.at[4])
+    for copy in (load_q, load_k, load_v, move_dec, move_part):
+        copy.start()
+    fill_diag(diag)
+    load_q.wait()
+    load_k.wait()
+    load_v.wait()
+    outs = prefill_block(qp[...], kbuf, vbuf, diag, kbuf.shape[0])
+    for h in range(STACK):
+        out[:, h * HEAD_DIM:(h + 1) * HEAD_DIM] = outs[h * TILE:(h + 1) * TILE]
+    store = pltpu.make_async_copy(out, pout_hbm.at[rest], sem.at[5])
+    store.start()
+    move_dec.wait()
+    move_part.wait()
+    store.wait()
 
 
 def kernel(
@@ -51,6 +96,8 @@
     res_len,
     pout_hbm,
     dout_hbm,
+    k_hbm,
+    v_hbm,
     qp,
     fresh,
     pool,
@@ -118,7 +165,7 @@
         pltpu.make_async_copy(qp_hbm, qp, load_sem.at[4]),
         pltpu.make_async_copy(res_hbm, res, load_sem.at[5]),
     ]
-    for one in loads:
+    for one in loads[:5]:
         one.start()
 
     loads[0].wait()
@@ -158,6 +205,7 @@
 
     loads[2].wait()
     loads[3].wait()
+    loads[5].start()
     ctx_len = lengths[me * (finished + 1) + finished]
     first_key = pool[0, table[finished, 0]][0:1]
     block = pool.shape[2]
@@ -174,24 +222,18 @@
     kbuf[MAXLEN:] = fresh[0]
     vbuf[MAXLEN:, :HEAD_DIM] = fresh[1]
     vbuf[MAXLEN:, HEAD_DIM:] = jnp.ones((seg, HEAD_DIM), BF16)
-    row = lax.broadcasted_iota(jnp.int32, (STACK * TILE, TILE), 0) % TILE
-    col = lax.broadcasted_iota(jnp.int32, (STACK * TILE, TILE), 1)
-    diag[...] = jnp.where(col <= row, 0.0, NEG_FILL)
+    fill_diag(diag)
+    keys_out = pltpu.make_async_copy(kbuf, k_hbm, out_sem.at[3])
+    keys_out.start()
+    values_out = pltpu.make_async_copy(vbuf, v_hbm, out_sem.at[4])
+    values_out.start()
     loads[4].wait()
 
     def prefill(i):
         rows = slice(i * TILE, (i + 1) * TILE)
-        span = MAXLEN + (i + 1) * TILE
-        cols = [slice(h * HEAD_DIM, (h + 1) * HEAD_DIM) for h in range(STACK)]
-        q = jnp.concatenate([qp[rows, c] for c in cols], axis=0)
-        s = dot_nt(q, kbuf[:span])
-        s = jnp.concatenate([s[:, :span - TILE], s[:, span - TILE:] + diag[...]], axis=1)
-        top = jnp.max(s, axis=1, keepdims=True)
-        p = jnp.exp2(s * SCALE - top * SCALE).astype(BF16)
-        o = dot_nn(p, vbuf[:span])
-        o = (o[:, :HEAD_DIM] / o[:, HEAD_DIM:]).astype(BF16)
+        outs = prefill_block(qp[rows], kbuf, vbuf, diag, MAXLEN + (i + 1) * TILE)
         for h in range(STACK):
-            pout[rows, cols[h]] = o[h * TILE:(h + 1) * TILE]
+            pout[rows, h * HEAD_DIM:(h + 1) * HEAD_DIM] = outs[h * TILE:(h + 1) * TILE]
 
     def out_rows(first, last, i):
         rows = pl.ds(first * TILE, (last - first) * TILE)
@@ -199,7 +241,8 @@
         copy.start()
         return copy
 
-    prefill(0)
+    for i in range(EARLY):
+        prefill(i)
 
     pl.semaphore_wait(barrier, groups)
 
@@ -234,9 +277,9 @@
     pack_recv[me] = pack_send[me]
 
 
-    for i in range(1, 5):
+    for i in range(EARLY, MIDDLE):
         prefill(i)
-    out_first = out_rows(0, 5, 0)
+    out_first = out_rows(0, MIDDLE, 0)
 
     loads[5].wait()
     q_copy.wait()
@@ -391,9 +434,9 @@
     step_stat[0] = jnp.broadcast_to(top, o.shape).reshape(rows3)
     step_stat[1] = jnp.broadcast_to(norm, o.shape).reshape(rows3)
 
-    for i in range(5, 8):
+    for i in range(MIDDLE, LAST):
         prefill(i)
-    out_second = out_rows(5, 8, 1)
+    out_second = out_rows(MIDDLE, LAST, 1)
 
     part_pair.wait()
     stat_pair.wait()
@@ -449,6 +492,8 @@
     out_first.wait()
     out_second.wait()
     out_dec.wait()
+    keys_out.wait()
+    values_out.wait()
 
 
 def per_device(*args):
@@ -468,7 +513,7 @@
         vmem(q_decode.shape, BF16),
         vmem(kv_steps.shape, BF16),
         vmem(kv_res.shape, BF16),
-        vmem(q_prefill.shape, BF16),
+        vmem((LAST * TILE, q_prefill.shape[1]), BF16),
         vmem(q_decode.shape, BF16),
         vmem((MAXLEN + seg, HEAD_DIM), BF16),
         vmem((MAXLEN + seg, 2 * HEAD_DIM), BF16),
@@ -491,7 +536,7 @@
         vmem((2, res_rows, q_rows, HEAD_DIM), F32),
         vmem((2, 2, res_rows, q_rows, HEAD_DIM), F32),
         pltpu.SemaphoreType.DMA((6,)),
-        pltpu.SemaphoreType.DMA((3,)),
+        pltpu.SemaphoreType.DMA((5,)),
         pltpu.SemaphoreType.DMA((groups,)),
         pltpu.SemaphoreType.DMA((groups,)),
         pltpu.SemaphoreType.DMA((groups,)),
@@ -501,14 +546,20 @@
     ]
     hbm = pl.BlockSpec(memory_space=pl.ANY)
     smem = pl.BlockSpec(memory_space=pltpu.SMEM)
-    return pl.pallas_call(
+    keys = jax.ShapeDtypeStruct((MAXLEN + seg, HEAD_DIM), BF16)
+    values = jax.ShapeDtypeStruct((MAXLEN + seg, 2 * HEAD_DIM), BF16)
+    pre_out = jax.ShapeDtypeStruct(q_prefill.shape, BF16)
+    dec_out = jax.ShapeDtypeStruct(q_decode.shape, BF16)
+    part, dec, k_all, v_all = pl.pallas_call(
         functools.partial(kernel, groups),
         out_shape=(
-            jax.ShapeDtypeStruct(q_prefill.shape, BF16),
-            jax.ShapeDtypeStruct(q_decode.shape, BF16),
+            jax.ShapeDtypeStruct((LAST * TILE, q_prefill.shape[1]), BF16),
+            dec_out,
+            keys,
+            values,
         ),
         in_specs=[hbm, hbm, hbm, smem, smem, smem, hbm, hbm, hbm, smem],
-        out_specs=(hbm, hbm),
+        out_specs=(hbm,) * 4,
         scratch_shapes=scratch,
         compiler_params=pltpu.CompilerParams(
             collective_id=0, has_side_effects=True, vmem_limit_bytes=56 * 2**20
@@ -517,6 +568,25 @@
             flops=8 * 10**9, bytes_accessed=21 * 10**6, transcendentals=14 * 10**6
         ),
     )(*args)
+    last = seg - LAST * TILE
+    return pl.pallas_call(
+        tail_kernel,
+        out_shape=(pre_out, dec_out),
+        in_specs=[hbm] * 5,
+        out_specs=(hbm, hbm),
+        scratch_shapes=[
+            vmem((last, q_prefill.shape[1]), BF16),
+            vmem(keys.shape, BF16),
+            vmem(values.shape, BF16),
+            vmem((last, q_prefill.shape[1]), BF16),
+            vmem((STACK * TILE, TILE), F32),
+            pltpu.SemaphoreType.DMA((6,)),
+        ],
+        compiler_params=pltpu.CompilerParams(vmem_limit_bytes=56 * 2**20),
+        cost_estimate=pl.CostEstimate(
+            flops=10**9, bytes_accessed=8 * 10**6, transcendentals=2 * 10**6
+        ),
+    )(q_prefill, k_all, v_all, part, dec)
 
 
 def solution(mesh):

time: 41 us -> 109 us (2.66)
  Pallas kernels: 36.2 us -> 108 us
  local copies, waits for them, and re-layouts: 3.93 us -> 0 us
    pallas_call x0 -> x1, Pallas kernels: none -> 72.6 us  [per_device(): pl.pallas_call(tail_kernel, out_shape=(pre_out, dec_out), in_specs=[hbm]...]
    unnamed x4 -> x0, local copies, waits for them, and re-layouts: 3.93 us -> none
    pallas_call x1, Pallas kernels: 36.2 us -> 35.1 us  [per_device(): pl.pallas_call(functools.partial(kernel, groups), out_shape=(jax.ShapeDty...]
where the time goes in v4:
time: 109 us
  Pallas kernels  108 us (99%)
    pallas_call x1, Pallas kernels, per_device(): pl.pallas_call(tail_kernel, out_shape=(pre_out, dec_out), in_specs=[hbm]...  72.6 us
    pallas_call x1, Pallas kernels, per_device(): pl.pallas_call(functools.partial(kernel, groups), out_shape=(jax.ShapeDty...  35.1 us

profile of v4, /device:TPU:1, one launch (start us, length us, event | category | flops | bytes accessed | tf_op | source)
XLA Modules:
  0.0 108.6 jit_solution(14627386288593109874)
XLA Ops:
  0.6 35.1 %shard_map.113 = (bf16[896,1024]{1,0:T(8,128)(2,1)}, bf16[64,4,1024]{2,1,0:T(4,128)(2,1)}, bf16[2048,128]{1,0:T(8,128)(2,1)}, bf16[2048,256]{1,0:T(8,128)(2,1)}) custom-call(bf16[1024,1024]{1,0:T(8,128)(2,1)} %qp_hbm.3, bf16[2,1024,128]{2,1,0:T(8,128)(2,1)} %fresh_hbm.1, bf16[2,208,64,128]{3,2,1,0:T(8,128)(2,1)} %pool_hbm.1, s32[13,16]{1,0:T(8,128)} %table.1, ...), custom_call_target="tpu_custom_call" | custom-call | flops 8000000000 | bytes 21000000 | tf_op jit(solution)/shard_map/pallas_call | solution.py:553
  35.8 72.6 %shard_map.114 = (bf16[1024,1024]{1,0:T(8,128)(2,1)}, bf16[64,4,1024]{2,1,0:T(4,128)(2,1)}) custom-call(bf16[1024,1024]{1,0:T(8,128)(2,1)} %qp_hbm.3, bf16[2048,128]{1,0:T(8,128)(2,1)} %get-tuple-element.6.k_hbm, bf16[2048,256]{1,0:T(8,128)(2,1)} %get-tuple-element.7.v_hbm, bf16[896,1024]{1,0:T(8,128)(2,1)} %get-tuple-element.8.part_hbm, ...), custom_call_target="tpu_custom_call" | custom-call | flops 1000000000 | bytes 8000000 | tf_op jit(solution)/shard_map/pallas_call | solution.py:572

commit v5 on v2

--- a/solution.py
+++ b/solution.py
@@ -18,6 +18,9 @@
 STACK = 8
 BATCH = 8
 FIN_BATCH = 4
+EARLY = 1
+MIDDLE = 5
+AHEAD = 0
 MESH = pl.DeviceIdType.MESH
 BF16 = jnp.bfloat16
 F32 = jnp.float32
@@ -35,6 +38,38 @@
     wide = x.astype(F32)
     parts = [wide[:, a * HEAD_DIM:(a + 1) * HEAD_DIM] for a in range(Q_PER_KV)]
     return jnp.concatenate(parts, axis=0).astype(BF16)
+
+
+def stacked(q_cols):
+    return jnp.concatenate(
+        [q_cols[:, h * HEAD_DIM:(h + 1) * HEAD_DIM] for h in range(STACK)], axis=0
+    )
+
+
+def causal_scores(q, keys, diag):
+    s = dot_nt(q, keys)
+    edge = s.shape[1] - TILE
+    if edge == 0:
+        return s + diag[...]
+    return jnp.concatenate([s[:, :edge], s[:, edge:] + diag[...]], axis=1)
+
+
+def weigh(s, top, values):
+    return dot_nn(jnp.exp2((s - top) * SCALE).astype(BF16), values)
+
+
+def row_max(s):
+    return jnp.max(s, axis=1, keepdims=True)
+
+
+def normalized(o):
+    return (o[:, :HEAD_DIM] / o[:, HEAD_DIM:]).astype(BF16)
+
+
+def fill_diag(diag):
+    row = lax.broadcasted_iota(jnp.int32, (STACK * TILE, TILE), 0) % TILE
+    col = lax.broadcasted_iota(jnp.int32, (STACK * TILE, TILE), 1)
+    diag[...] = jnp.where(col <= row, 0.0, NEG_FILL)
 
 
 def kernel(
@@ -62,6 +97,8 @@
     kbuf,
     vbuf,
     diag,
+    ahead_sum,
+    ahead_top,
     q_pair,
     pack_send,
     pack_recv,
@@ -118,11 +155,12 @@
         pltpu.make_async_copy(qp_hbm, qp, load_sem.at[4]),
         pltpu.make_async_copy(res_hbm, res, load_sem.at[5]),
     ]
-    for one in loads:
-        one.start()
+    for i in (0, 1, 2, 4):
+        loads[i].start()
 
     loads[0].wait()
     loads[1].wait()
+    loads[3].start()
 
     def relay_res(r, carry):
         q_pair[side, r] = heads_to_rows(qd[r])
@@ -157,7 +195,21 @@
     lax.fori_loop(0, res_rows // per_tile, gather_steps, 0, unroll=2)
 
     loads[2].wait()
+    kbuf[MAXLEN:] = fresh[0]
+    vbuf[MAXLEN:, :HEAD_DIM] = fresh[1]
+    vbuf[MAXLEN:, HEAD_DIM:] = jnp.ones((seg, HEAD_DIM), BF16)
+    fill_diag(diag)
+    loads[4].wait()
+
+    for i in range(AHEAD):
+        span = (i + 1) * TILE
+        s = causal_scores(stacked(qp[i * TILE:span]), kbuf[MAXLEN:MAXLEN + span], diag)
+        top = row_max(s)
+        ahead_top[i] = jnp.broadcast_to(top, (STACK * TILE, HEAD_DIM))
+        ahead_sum[i] = weigh(s, top, vbuf[MAXLEN:MAXLEN + span])
+
     loads[3].wait()
+    loads[5].start()
     ctx_len = lengths[me * (finished + 1) + finished]
     first_key = pool[0, table[finished, 0]][0:1]
     block = pool.shape[2]
@@ -171,27 +223,34 @@
             valid, pool[1, blk].astype(F32), 0.0
         ).astype(BF16)
         vbuf[b * block:(b + 1) * block, HEAD_DIM:] = jnp.where(valid, 1.0, 0.0).astype(BF16)
-    kbuf[MAXLEN:] = fresh[0]
-    vbuf[MAXLEN:, :HEAD_DIM] = fresh[1]
-    vbuf[MAXLEN:, HEAD_DIM:] = jnp.ones((seg, HEAD_DIM), BF16)
-    row = lax.broadcasted_iota(jnp.int32, (STACK * TILE, TILE), 0) % TILE
-    col = lax.broadcasted_iota(jnp.int32, (STACK * TILE, TILE), 1)
-    diag[...] = jnp.where(col <= row, 0.0, NEG_FILL)
-    loads[4].wait()
-
-    def prefill(i):
+
+    def prefill_scores(i):
+        q = stacked(qp[i * TILE:(i + 1) * TILE])
+        if i < AHEAD:
+            return dot_nt(q, kbuf[:MAXLEN])
+        return causal_scores(q, kbuf[:MAXLEN + (i + 1) * TILE], diag)
+
+    def prefill_rest(i, s):
         rows = slice(i * TILE, (i + 1) * TILE)
-        span = MAXLEN + (i + 1) * TILE
-        cols = [slice(h * HEAD_DIM, (h + 1) * HEAD_DIM) for h in range(STACK)]
-        q = jnp.concatenate([qp[rows, c] for c in cols], axis=0)
-        s = dot_nt(q, kbuf[:span])
-        s = jnp.concatenate([s[:, :span - TILE], s[:, span - TILE:] + diag[...]], axis=1)
-        top = jnp.max(s, axis=1, keepdims=True)
-        p = jnp.exp2(s * SCALE - top * SCALE).astype(BF16)
-        o = dot_nn(p, vbuf[:span])
-        o = (o[:, :HEAD_DIM] / o[:, HEAD_DIM:]).astype(BF16)
+        if i < AHEAD:
+            top = jnp.maximum(jnp.broadcast_to(row_max(s), (STACK * TILE, HEAD_DIM)), ahead_top[i])
+            w = jnp.exp2((ahead_top[i] - top) * SCALE)
+            o = weigh(s, top[:, :1], vbuf[:MAXLEN])
+            o = o + ahead_sum[i] * jnp.concatenate([w, w], axis=1)
+        else:
+            o = weigh(s, row_max(s), vbuf[:MAXLEN + (i + 1) * TILE])
+        outs = normalized(o)
         for h in range(STACK):
-            pout[rows, cols[h]] = o[h * TILE:(h + 1) * TILE]
+            pout[rows, h * HEAD_DIM:(h + 1) * HEAD_DIM] = outs[h * TILE:(h + 1) * TILE]
+
+    def prefill(first, last, s=None, after=False):
+        if s is None:
+            s = prefill_scores(first)
+        for i in range(first, last):
+            ahead = prefill_scores(i + 1) if after or i + 1 < last else None
+            prefill_rest(i, s)
+            s = ahead
+        return s
 
     def out_rows(first, last, i):
         rows = pl.ds(first * TILE, (last - first) * TILE)
@@ -199,7 +258,7 @@
         copy.start()
         return copy
 
-    prefill(0)
+    scores = prefill(0, EARLY, after=True)
 
     pl.semaphore_wait(barrier, groups)
 
@@ -234,9 +293,8 @@
     pack_recv[me] = pack_send[me]
 
 
-    for i in range(1, 5):
-        prefill(i)
-    out_first = out_rows(0, 5, 0)
+    prefill(EARLY, MIDDLE, scores)
+    out_first = out_rows(0, MIDDLE, 0)
 
     loads[5].wait()
     q_copy.wait()
@@ -279,7 +337,9 @@
         return tops, norms
 
     zeros = jnp.zeros((q_rows, HEAD_DIM), F32)
-    tops, norms = lax.fori_loop(0, res_rows // BATCH, resident_rows, (zeros, zeros))
+    tops, norms = zeros, zeros
+    for i in range(res_rows // BATCH):
+        tops, norms = resident_rows(i, (tops, norms))
     stat_send[0] = tops
     stat_send[1] = norms
     part_pair = pair_copy(part_send.at[1 - side], part_recv, 1)
@@ -345,6 +405,7 @@
             o = dot_nn(p.astype(BF16), values) + dot_nn(p2.astype(BF16), v2)
             ans[f] = (o / l).astype(BF16)
 
+    next_scores = prefill_scores(MIDDLE)
     for first in range(0, finished, FIN_BATCH):
         finished_rows(range(first, min(first + FIN_BATCH, finished)))
 
@@ -391,12 +452,12 @@
     step_stat[0] = jnp.broadcast_to(top, o.shape).reshape(rows3)
     step_stat[1] = jnp.broadcast_to(norm, o.shape).reshape(rows3)
 
-    for i in range(5, 8):
-        prefill(i)
-    out_second = out_rows(5, 8, 1)
-
+    blocks = seg // TILE
+    scores = prefill(MIDDLE, blocks - 1, next_scores, after=True)
     part_pair.wait()
     stat_pair.wait()
+    prefill_rest(blocks - 1, scores)
+    out_second = out_rows(MIDDLE, blocks, 1)
 
     def put_row(dst_row, x):
         for a in range(Q_PER_KV):
@@ -415,7 +476,12 @@
         put_row(r, x / norm)
         return carry
 
-    lax.fori_loop(0, res_rows, merge, 0, unroll=4)
+    for r in range(res_rows):
+        merge(r, 0)
+    out_res = pltpu.make_async_copy(
+        dout.at[pl.ds(0, res_rows)], dout_hbm.at[pl.ds(0, res_rows)], out_sem.at[2]
+    )
+    out_res.start()
 
     def wait_answer(d, carry):
         peer = (me + d) % groups
@@ -444,11 +510,13 @@
         return carry
 
     lax.fori_loop(0, groups, arrive, 0, unroll=2)
-    out_dec = pltpu.make_async_copy(dout, dout_hbm, out_sem.at[2])
-    out_dec.start()
+    arrived = pl.ds(res_rows, groups * CAPACITY)
+    out_arr = pltpu.make_async_copy(dout.at[arrived], dout_hbm.at[arrived], out_sem.at[3])
+    out_arr.start()
     out_first.wait()
     out_second.wait()
-    out_dec.wait()
+    out_res.wait()
+    out_arr.wait()
 
 
 def per_device(*args):
@@ -473,6 +541,8 @@
         vmem((MAXLEN + seg, HEAD_DIM), BF16),
         vmem((MAXLEN + seg, 2 * HEAD_DIM), BF16),
         vmem((STACK * TILE, TILE), F32),
+        vmem((max(AHEAD, 1), STACK * TILE, 2 * HEAD_DIM), F32),
+        vmem((max(AHEAD, 1), STACK * TILE, HEAD_DIM), F32),
         vmem((2, res_rows, q_rows, HEAD_DIM), BF16),
         vmem((groups, PACK, HEAD_DIM), BF16),
         vmem((groups, PACK, HEAD_DIM), BF16),
@@ -491,7 +561,7 @@
         vmem((2, res_rows, q_rows, HEAD_DIM), F32),
         vmem((2, 2, res_rows, q_rows, HEAD_DIM), F32),
         pltpu.SemaphoreType.DMA((6,)),
-        pltpu.SemaphoreType.DMA((3,)),
+        pltpu.SemaphoreType.DMA((4,)),
         pltpu.SemaphoreType.DMA((groups,)),
         pltpu.SemaphoreType.DMA((groups,)),
         pltpu.SemaphoreType.DMA((groups,)),

time: 41 us -> 38.5 us (0.939)
  Pallas kernels: 36.2 us -> 33.7 us
    pallas_call x1, Pallas kernels: 36.2 us -> 33.7 us  [per_device(): pl.pallas_call(functools.partial(kernel, groups), out_shape=(jax.ShapeDty...]
where the time goes in v5:
time: 38.5 us; the launch traced here: 38.3 us
  Pallas kernels  33.7 us (88%)
  local copies, waits for them, and re-layouts  3.93 us (10%)
  between operations  0.65 us (2%)
    pallas_call x1, Pallas kernels, per_device(): pl.pallas_call(functools.partial(kernel, groups), out_shape=(jax.ShapeDty...  33.7 us
    unnamed x4, local copies, waits for them, and re-layouts  3.93 us

profile of v5, /device:TPU:1, one launch (start us, length us, event | category | flops | bytes accessed | tf_op | source)
XLA Modules:
  0.0 38.3 jit_solution(9427735729436109712)
XLA Ops:
  0.6 33.7 %shard_map.113 = (bf16[1024,1024]{1,0:T(8,128)(2,1)}, bf16[64,4,1024]{2,1,0:T(4,128)(2,1)}) custom-call(bf16[1024,1024]{1,0:T(8,128)(2,1)} %qp_hbm.1, bf16[2,1024,128]{2,1,0:T(8,128)(2,1)} %fresh_hbm.1, bf16[2,208,64,128]{3,2,1,0:T(8,128)(2,1)} %pool_hbm.1, s32[13,16]{1,0:T(8,128)} %table.1, s32[208]{0:T(256)} %lengths.1, s32[192]{0:T(256)} %owners.1, ...), custom_call_target="tpu_custom_call" | custom-call | flops 8000000000 | bytes 21000000 | tf_op jit(solution)/shard_map/pallas_call | solution.py:574
  34.3 0.0 copy-start
  34.3 3.1 %copy.14 = bf16[1024,1024]{1,0:T(8,128)(2,1)} copy(bf16[1024,1024]{1,0:T(8,128)(2,1)} %get-tuple-element.4) | data formatting | bytes 4194304
  37.5 0.0 copy-done
  37.5 0.8 %copy.15 = bf16[64,4,1024]{2,1,0:T(4,128)(2,1)} copy(bf16[64,4,1024]{2,1,0:T(4,128)(2,1)S(1)} %copy-done) | data formatting | bytes 1048576
Async XLA Ops:
  34.3 3.1 %copy-start = (bf16[64,4,1024]{2,1,0:T(4,128)(2,1)S(1)}, bf16[64,4,1024]{2,1,0:T(4,128)(2,1)}, u32[]{:S(2)}) copy-start(bf16[64,4,1024]{2,1,0:T(4,128)(2,1)} %get-tuple-element.5) | copy-start | bytes 1572868
